TPU v7x, 256 devices: a whole 4x4x8 slice. The times are simulated.
256 devices in a mesh: replica: 4 (over z_hi), fsdp: 64 (over z_lo, y, x, core).
Axes of the slice: x: 4, y: 4, z: 8 (z_hi: 4, z_lo: 2; z = z_hi * 2 + z_lo), core: 2. Of those that a mesh axis runs over, the one named last changes fastest.
Arguments:
- hidden: bfloat16 [4, 24576, 8192], P('replica', 'fsdp'), may hold values from -6 to 6
- master: float32 [4, 8192, 512], P('replica', 'fsdp'), may hold values from -0.0625 to 0.0625
- moment_first: float32 [4, 8192, 512], P('replica', 'fsdp'), may hold values from -4 to 4
- moment_second: float32 [4, 8192, 512], P('replica', 'fsdp'), may hold values from 0.05 to 2
- key_grad: bfloat16 [4, 24576, 512], P('replica', 'fsdp'), may hold values from -0.09375 to 0.09375
- frag_global: float32 [2, 8388608], P(None, 'fsdp'), may hold values from -6 to 6
- frag_local: float32 [4, 2, 8388608], P('replica', None, 'fsdp'), may hold values from -6 to 6
- frag_moment: float32 [2, 8388608], P(None, 'fsdp'), may hold values from -6 to 6
- frag_index: int32 [1], replicated, may hold values from 0 to 1
Outputs:
- new_master: float32 [4, 8192, 512], P('replica', 'fsdp')
- new_first: float32 [4, 8192, 512], P('replica', 'fsdp')
- new_second: float32 [4, 8192, 512], P('replica', 'fsdp')
- outer_global: float32 [8388608], P('fsdp')
- outer_moment: float32 [8388608], P('fsdp')
- mixed_local: float32 [4, 8388608], P('replica', 'fsdp')
All inputs are finite; a program needn't handle non-finite values.
Results may differ from a plain program's by a relative error of at most 0.0011.
Values may be sent and summed in bfloat16 or wider, within the bound.
A program may use at most 128 MiB of HBM per device.

v0:
```python
import jax
import jax.numpy as jnp
from jax import lax
from jax.sharding import PartitionSpec as P

HEAD = 128


def norm_backward(keys, grads):
    count = keys.shape[0]
    shaped = keys.reshape(count, -1, HEAD)
    inverse = lax.rsqrt(jnp.mean(shaped * shaped, axis=-1, keepdims=True) + 1e-06)
    normed = shaped * inverse
    upstream = grads.astype(jnp.float32).reshape(count, -1, HEAD)
    result = inverse * (upstream - normed * jnp.mean(upstream * normed, axis=-1, keepdims=True))
    return result.reshape(count, -1).astype(jnp.bfloat16)


def adamw(weights, first, second, grad):
    first_new = 0.9 * first + 0.1 * grad
    second_new = 0.95 * second + 0.05 * grad * grad
    first_hat = first_new / (1.0 - 0.9**10)
    second_hat = second_new / (1.0 - 0.95**10)
    weights_new = weights - 0.01 * (first_hat / (jnp.sqrt(second_hat) + 1e-08) + 0.1 * weights)
    return (weights_new, first_new, second_new)


def shards(
    hidden,
    master,
    moment_first,
    moment_second,
    key_grad,
    frag_global,
    frag_local,
    frag_moment,
    frag_index,
):
    inputs = hidden[0]
    weights = master[0]
    weight_bf = weights.astype(jnp.bfloat16)
    columns = inputs
    keys = jnp.dot(
        columns,
        lax.all_gather(weight_bf, "fsdp", axis=0, tiled=True),
        preferred_element_type=jnp.float32,
    )
    key_delta = norm_backward(keys, key_grad[0])
    columns = inputs
    grad = lax.psum_scatter(
        jnp.dot(columns.T, key_delta, preferred_element_type=jnp.float32),
        "fsdp",
        scatter_dimension=0,
        tiled=True,
    )
    weights_new, first_new, second_new = adamw(weights, moment_first[0], moment_second[0], grad)
    chosen = frag_index[0]
    glob = lax.dynamic_index_in_dim(frag_global, chosen, 0, keepdims=False)
    moment = lax.dynamic_index_in_dim(frag_moment, chosen, 0, keepdims=False)
    local = lax.dynamic_index_in_dim(frag_local[0], chosen, 0, keepdims=False)
    groups = lax.axis_size("replica")
    delta = lax.psum(glob - local, "replica") / groups
    outer_moment = 0.9 * moment + delta
    outer_global = glob - 0.7 * (0.9 * outer_moment + delta)
    mixed_local = 0.5 * local + 0.5 * outer_global
    return (
        weights_new[None],
        first_new[None],
        second_new[None],
        outer_global,
        outer_moment,
        mixed_local[None],
    )


def solution(mesh):
    placed = (
        P("replica", "fsdp", None),
        P("replica", "fsdp", None),
        P("replica", "fsdp", None),
        P("replica", "fsdp", None),
        P("replica", "fsdp", None),
        P(None, "fsdp"),
        P("replica", None, "fsdp"),
        P(None, "fsdp"),
        P(),
    )
    return jax.shard_map(
        shards,
        mesh=mesh,
        in_specs=placed,
        out_specs=(
            P("replica", "fsdp", None),
            P("replica", "fsdp", None),
            P("replica", "fsdp", None),
            P("fsdp"),
            P("fsdp"),
            P("replica", "fsdp"),
        ),
        check_vma=False,
    )
```

profile of v0, /device:TPU:32, one launch (start us, length us, event | category | flops | bytes accessed | tf_op | source)
XLA Modules:
  0.0 487.8 jit_solution(2648470338139009136)
XLA Ops:
  8.0 0.0 all-gather.2.cloned.1.call-start
  8.1 1.1 copy.15
  9.2 0.7 bitcast_convert_fusion
  9.9 0.0 all-reduce.2.cloned.1.call-start
  10.6 0.5 constant_dynamic-slice_fusion
  11.1 1.7 constant_dynamic-slice_fusion.1
  12.8 0.8 sub.14
  13.6 0.0 reduce-scatter.2.cloned.1.call-start
  13.7 1.2 copy.17
  14.9 130.7 %all-gather.2.cloned.1.call-done = bf16[8192,512]{0,1:T(8,128)(2,1)} async-done(((bf16[128,512]{0,1:T(8,128)(2,1)}), bf16[8192,512]{0,1:T(8,128)(2,1)}) %all-gather.2.cloned.1.call-update) | async-done | bytes 8388624 | tf_op jit(solution)/shard_map/all_gather | solution.py:45
  145.6 9.8 %multiply_reduce_fusion.1 = (f32[384,4]{0,1:T(4,128)S(1)}, f32[384,4,128]{0,2,1:T(8,128)S(1)}) fusion(bf16[4,128,8192]{2,1,0:T(8,128)(2,1)} %bitcast.66, bf16[1,384,8192]{2,1,0:T(8,128)(2,1)} %param.9), kind=kOutput, calls=%fused_computation.6 | convolution fusion | flops 3221617152 | bytes 15472640 | tf_op jit(solution)/shard_map/dot_general | solution.py:43
  155.4 0.1 multiply_reduce_fusion
  155.5 0.1 multiply_convert_fusion
  155.7 8.1 %convolution_bitcast_fusion = f32[8192,512]{0,1:T(8,128)} fusion(bf16[384,512]{0,1:T(8,128)(2,1)S(1)} %bitcast.64, bf16[1,384,8192]{2,1,0:T(8,128)(2,1)S(1)} %bitcast.58), kind=kOutput, calls=%fused_computation | convolution fusion | flops 3221225472 | bytes 23461888 | tf_op jit(solution)/shard_map/dot_general | solution.py:51
  163.8 0.9 copy-done.1
  164.7 0.1 copy.18
  164.9 0.1 copy.16
  165.0 1.9 dynamic-slice_multiply_fusion
  167.0 2.3 add_multiply_fusion
  169.3 307.4 %reduce-scatter.2.cloned.1.call-done = f32[128,512]{0,1:T(8,128)} async-done(((f32[8192,512]{0,1:T(8,128)}), f32[128,512]{0,1:T(8,128)}) %reduce-scatter.2.cloned.1.call-update) | async-done | bytes 262160 | tf_op jit(solution)/shard_map/reduce_scatter | solution.py:50
  476.7 1.2 fusion.8
  477.9 0.8 copy.19
  478.7 0.8 copy.20
  479.6 0.8 copy.21
  (16 shorter events, 0.1 us)
Async XLA Ops:
  8.0 2.6 copy-start
  8.0 137.6 %all-gather.2.cloned.1.call-start = ((), (), s32[]{:S(2)}) async-start(), calls=%async_computation.1 | async-start | bytes 8519680 | tf_op jit(solution)/shard_map/all_gather | solution.py:45
  9.9 157.1 %all-reduce.2.cloned.1.call-start = ((), (), s32[]{:S(2)}) async-start(), calls=%async_computation.3 | async-start | bytes 1048576 | tf_op jit(solution)/shard_map/psum | solution.py:62
  13.6 463.1 %reduce-scatter.2.cloned.1.call-start = ((), (), s32[]{:S(2)}) async-start(), calls=%async_computation.2 | async-start | bytes 17039360 | tf_op jit(solution)/shard_map/reduce_scatter | solution.py:50
  145.6 10.1 %slice-start = ((s8[6291456]{0:T(1024)(128)(4,1)}), s8[4194304]{0:T(1024)(128)(4,1)S(1)}, s32[]{:S(2)}) async-start(s8[6291456]{0:T(1024)(128)(4,1)} %bitcast.57), calls=%async_computation.4 | async-start | bytes 8388608
  145.6 10.1 %slice-start.1 = ((s8[6291456]{0:T(1024)(128)(4,1)}), s8[2097152]{0:T(1024)(128)(4,1)S(1)}, s32[]{:S(2)}) async-start(s8[6291456]{0:T(1024)(128)(4,1)} %bitcast.57), calls=%async_computation.5 | async-start | bytes 4194304
  163.8 0.9 copy-start.1
  163.8 1.1 copy-start.2
Sparse Core Ops, SparseCore 0:
  11.2 134.3 all-gather.1
  163.9 312.7 reduce-scatter.1
Sparse Core Ops, SparseCore 1:
  13.7 56.5 all-reduce.1
where the time goes:
time: 489 us; the launch traced here: 488 us
  waiting for transfers between devices  438 us (90%)
  matrix products  17.9 us (4%)
  between operations  16.3 us (3%)
  local copies, waits for them, and re-layouts  8.14 us (2%)
  other arithmetic  7.2 us (1%)
    reduce_scatter x1, waiting for transfers between devices, shards(): lax.psum_scatter(jnp.dot(columns.T, key_delta, preferred_element_type=jnp...  307 us
    all_gather x1, waiting for transfers between devices, shards(): lax.all_gather(weight_bf, 'fsdp', axis=0, tiled=True)  131 us
  transfers between devices with their start and end apart: 3, of which 2 were waited for; matrix products, arithmetic and copies ran while one was open for 5% of the time, Pallas kernels for 0%

commit v1 on v0

v1 whole, which is shorter than its diff:
```python
import functools

import jax
import jax.numpy as jnp
from jax import lax
from jax.experimental import pallas as pl
from jax.experimental.pallas import tpu as pltpu
from jax.sharding import PartitionSpec as P

MESH = pl.DeviceIdType.MESH
HEAD = 128
PARTS = 2
WIDE = 256
TOK = 384
ROWS = 128
MESSAGES = 256


def adamw(weights, first, second, grad):
    first_new = 0.9 * first + 0.1 * grad
    second_new = 0.95 * second + 0.05 * grad * grad
    first_hat = first_new / (1.0 - 0.9**10)
    second_hat = second_new / (1.0 - 0.95**10)
    weights_new = weights - 0.01 * (first_hat / (jnp.sqrt(second_hat) + 1e-08) + 0.1 * weights)
    return (weights_new, first_new, second_new)


def norm_backward(keys, upstream):
    inverse = lax.rsqrt(jnp.mean(keys * keys, axis=-1, keepdims=True) + 1e-06)
    normed = keys * inverse
    return inverse * (upstream - normed * jnp.mean(upstream * normed, axis=-1, keepdims=True))


def kernel(
    hidden,
    master,
    key_grad,
    diff,
    grad_out,
    delta_out,
    hid,
    wts,
    acc,
    acc_in,
    dlt,
    stage,
    stage_in,
    row,
    final,
    z_stage,
    z_in,
    rep_in,
    send_sem,
    recv_sem,
    hid_sem,
):
    r = lax.axis_index("replica")
    f = lax.axis_index("fsdp")
    z, y, x, c = f // 32, (f // 8) % 4, (f // 2) % 4, f % 2

    def at(zz, yy, xx, cc):
        return (r, zz * 32 + (yy % 4) * 8 + (xx % 4) * 2 + cc)

    a_up, a_down = at(z, y + z, x + 1 - z, c), at(z, y + 4 - z, x + 3 + z, c)
    b_up, b_down = at(z, y + 1 - z, x + z, c), at(z, y + 3 + z, x + 4 - z, c)
    over_z, sibling = at(1 - z, y, x, c), at(z, y, x, 1 - c)
    reps = [((r + k) % 4, f) for k in (1, 2, 3)]
    ways = (((a_up, a_down), (b_up, b_down)), ((b_up, b_down), (a_up, a_down)))

    barrier = pltpu.get_barrier_semaphore()
    peers = [a_up, a_down, b_up, b_down, over_z, sibling, *reps]
    for peer in peers:
        pl.semaphore_signal(barrier, inc=1, device_id=peer, device_id_type=MESH)

    wts[0, 0] = master[:, :WIDE].astype(jnp.bfloat16)
    wts[1, 0] = master[:, WIDE:].astype(jnp.bfloat16)
    pl.semaphore_wait(barrier, len(peers))

    sent = {}

    def send(name, src, dst, to):
        n = len(sent)
        copy = pltpu.make_async_remote_copy(
            src_ref=src,
            dst_ref=dst,
            send_sem=send_sem.at[n],
            recv_sem=recv_sem.at[n],
            device_id=to,
            device_id_type=MESH,
        )
        copy.start()
        sent[name] = copy

    def arrived(*name):
        sent[name].wait_recv()

    def slot(h, t, s, q):
        return wts.at[h, 16 * t + 4 * s + q]

    lower, upper = pl.ds(0, ROWS // 2), pl.ds(ROWS // 2, ROWS // 2)

    def over_second(h, t, q):
        (_, _), (up, down) = ways[t]
        src = slot(h, t, 0, q)
        send(("s+", h, t, q), src, slot(h, t, 3, q), up)
        send(("s-", h, t, q), src, slot(h, t, 1, q), down)

    def gather_own(h, t):
        (up, down), _ = ways[t]
        if t == 1:
            arrived("z", h)
        src = slot(h, t, 0, 0)
        send(("f+", h, t), src, slot(h, t, 0, 3), up)
        send(("f-", h, t), src, slot(h, t, 0, 1), down)
        over_second(h, t, 0)

    def gather_next(h, t):
        (up, down), _ = ways[t]
        arrived("f+", h, t)
        send(("ff+", h, t), slot(h, t, 0, 3).at[lower], slot(h, t, 0, 2).at[lower], up)
        arrived("f-", h, t)
        send(("ff-", h, t), slot(h, t, 0, 1).at[upper], slot(h, t, 0, 2).at[upper], down)
        over_second(h, t, 3)
        over_second(h, t, 1)

    def gather_far(h, t):
        arrived("ff+", h, t)
        arrived("ff-", h, t)
        over_second(h, t, 2)

    def gather_pass(h, t, q):
        _, (up, down) = ways[t]
        arrived("s+", h, t, q)
        send(("ss+", h, t, q), slot(h, t, 3, q).at[lower], slot(h, t, 2, q).at[lower], up)
        arrived("s-", h, t, q)
        send(("ss-", h, t, q), slot(h, t, 1, q).at[upper], slot(h, t, 2, q).at[upper], down)

    def keys_add(h, t, s):
        if s == 2:
            for q in range(4):
                arrived("ss+", h, t, q)
                arrived("ss-", h, t, q)
        first = 16 * t + 4 * s
        part = jnp.dot(
            hid[:, first * ROWS : (first + 4) * ROWS],
            wts[h, first : first + 4].reshape(4 * ROWS, WIDE),
            preferred_element_type=jnp.float32,
        )
        if (t, s) == (0, 0):
            acc[h] = part
        else:
            acc[h] += part

    def keys_swap(h):
        send(("keys", h), acc.at[h, pl.ds(TOK, TOK)], acc_in.at[h], sibling)

    def deltas(h):
        arrived("keys", h)
        for n in range(WIDE // HEAD):
            cols = slice(n * HEAD, (n + 1) * HEAD)
            keys = acc[h, :TOK, cols] + acc_in[h, :, cols]
            at_col = h * WIDE + n * HEAD
            up = key_grad[:, at_col : at_col + HEAD].astype(jnp.float32)
            dlt[h, n * HEAD : (n + 1) * HEAD, :TOK] = norm_backward(keys, up).T.astype(jnp.bfloat16)
        send(("delta", h), dlt.at[h, :, pl.ds(0, TOK)], dlt.at[h, :, pl.ds(TOK, TOK)], sibling)

    low, high = slice(0, WIDE // 2), slice(WIDE // 2, WIDE)

    def grad_row(h, t, s):
        first = 16 * t + 4 * s
        return jnp.dot(
            dlt[h], hid[:, first * ROWS : (first + 4) * ROWS], preferred_element_type=jnp.float32
        )

    def row_send(name, h, t, s, half, to):
        n = 0 if half is low else WIDE // 2
        send(
            (name, h, t),
            stage.at[h, t, s, pl.ds(n, WIDE // 2), :],
            stage_in.at[h, t, s, pl.ds(n, WIDE // 2), :],
            to,
        )

    def scatter_far(h, t):
        _, (up, down) = ways[t]
        stage[h, t, 2] = grad_row(h, t, 2).astype(jnp.bfloat16)
        row_send("rf+", h, t, 2, low, up)
        row_send("rf-", h, t, 2, high, down)

    def scatter_near(h, t):
        _, (up, down) = ways[t]
        g1 = grad_row(h, t, 1)
        stage[h, t, 1, high, :] = g1[high].astype(jnp.bfloat16)
        row_send("r+h", h, t, 1, high, up)
        g3 = grad_row(h, t, 3)
        stage[h, t, 3, low, :] = g3[low].astype(jnp.bfloat16)
        row_send("r-l", h, t, 3, low, down)
        arrived("rf+", h, t)
        stage[h, t, 1, low, :] = (g1[low] + stage_in[h, t, 2, low, :].astype(jnp.float32)).astype(jnp.bfloat16)
        row_send("r+l", h, t, 1, low, up)
        arrived("rf-", h, t)
        stage[h, t, 3, high, :] = (g3[high] + stage_in[h, t, 2, high, :].astype(jnp.float32)).astype(jnp.bfloat16)
        row_send("r-h", h, t, 3, high, down)

    def scatter_own(h, t):
        g0 = grad_row(h, t, 0)
        for name in ("r+h", "r-l", "r+l", "r-h"):
            arrived(name, h, t)
        row[h, t] = g0 + stage_in[h, t, 1].astype(jnp.float32) + stage_in[h, t, 3].astype(jnp.float32)

    def one_send(name, h, t, q, half, to):
        n = 0 if half is low else WIDE // 2
        cols = pl.ds(q * ROWS, ROWS)
        send(
            (name, h, t),
            stage.at[h, t, 0, pl.ds(n, WIDE // 2), cols],
            stage_in.at[h, t, 0, pl.ds(n, WIDE // 2), cols],
            to,
        )

    def cols_of(q):
        return slice(q * ROWS, (q + 1) * ROWS)

    def first_far(h, t):
        (up, down), _ = ways[t]
        stage[h, t, 0, :, cols_of(2)] = row[h, t, :, cols_of(2)].astype(jnp.bfloat16)
        one_send("cf+", h, t, 2, low, up)
        one_send("cf-", h, t, 2, high, down)
        stage[h, t, 0, high, cols_of(1)] = row[h, t, high, cols_of(1)].astype(jnp.bfloat16)
        one_send("c+h", h, t, 1, high, up)
        stage[h, t, 0, low, cols_of(3)] = row[h, t, low, cols_of(3)].astype(jnp.bfloat16)
        one_send("c-l", h, t, 3, low, down)

    def first_near(h, t):
        (up, down), _ = ways[t]
        arrived("cf+", h, t)
        got = stage_in[h, t, 0, low, cols_of(2)].astype(jnp.float32)
        stage[h, t, 0, low, cols_of(1)] = (row[h, t, low, cols_of(1)] + got).astype(jnp.bfloat16)
        one_send("c+l", h, t, 1, low, up)
        arrived("cf-", h, t)
        got = stage_in[h, t, 0, high, cols_of(2)].astype(jnp.float32)
        stage[h, t, 0, high, cols_of(3)] = (row[h, t, high, cols_of(3)] + got).astype(jnp.bfloat16)
        one_send("c-h", h, t, 3, high, down)

    def first_own(h, t):
        for name in ("c+h", "c-l", "c+l", "c-h"):
            arrived(name, h, t)
        got = stage_in[h, t, 0, :, cols_of(1)].astype(jnp.float32) + stage_in[h, t, 0, :, cols_of(3)].astype(jnp.float32)
        total = row[h, t, :, cols_of(0)] + got
        if t == 1:
            z_stage[h] = total
            send(("gz", h), z_stage.at[h], z_in.at[h], over_z)
        else:
            final[h] = total

    def finish(h):
        arrived("gz", h)
        grad_out[h * WIDE : (h + 1) * WIDE, :] = final[h] + z_in[h]

    def replicas_start():
        for k, to in zip((1, 2, 3), reps):
            quarter = pl.ds(((r + k) % 4) * 256, 256)
            send(("rep", k), diff.at[quarter], rep_in.at[k - 1], to)

    def replicas_sum():
        for k in (1, 2, 3):
            arrived("rep", k)
        mine = pl.ds(r * 256, 256)
        delta_out[mine, :] = (diff[mine, :] + rep_in[0] + rep_in[1] + rep_in[2]) * 0.25
        for k, to in zip((1, 2, 3), reps):
            send(("rep out", k), delta_out.at[mine], delta_out.at[mine], to)

    for h in range(PARTS):
        send(("z", h), slot(h, 0, 0, 0), slot(h, 1, 0, 0), over_z)
        gather_own(h, 0)

    @pl.loop(0, 32)
    def _(n):
        t, s, q = n // 16, (n // 4) % 4, n % 4
        plane = (z + t) % 2
        yy = (y + s * (1 - plane) + q * plane) % 4
        xx = (x + q * (1 - plane) + s * plane) % 4
        chip = plane * 16 + yy * 4 + xx
        here = pl.ds(pl.multiple_of(n * ROWS, ROWS), ROWS)
        mine = pl.ds(pl.multiple_of((2 * chip + c) * ROWS, ROWS), ROWS)
        other = pl.ds(pl.multiple_of((2 * chip + 1 - c) * ROWS, ROWS), ROWS)
        pltpu.make_async_copy(hidden.at[:, mine], hid.at[pl.ds(0, TOK), here], hid_sem.at[0]).start()
        pltpu.make_async_remote_copy(
            src_ref=hidden.at[:, other],
            dst_ref=hid.at[pl.ds(TOK, TOK), here],
            send_sem=hid_sem.at[1],
            recv_sem=hid_sem.at[2],
            device_id=sibling,
            device_id_type=MESH,
        ).start()

    def hidden_wait():
        mine, theirs = hid.at[pl.ds(0, TOK)], hid.at[pl.ds(TOK, TOK)]
        pltpu.make_async_copy(mine, mine, hid_sem.at[0]).wait()
        pltpu.make_async_copy(mine, mine, hid_sem.at[1]).wait()
        pltpu.make_async_copy(theirs, theirs, hid_sem.at[2]).wait()

    def step1(h):
        gather_next(h, 0)
        gather_own(h, 1)
        gather_pass(h, 0, 0)

    def step2(h):
        gather_far(h, 0)
        gather_next(h, 1)
        gather_pass(h, 0, 3)
        gather_pass(h, 0, 1)
        gather_pass(h, 1, 0)

    def step3(h):
        gather_far(h, 1)
        gather_pass(h, 0, 2)
        gather_pass(h, 1, 3)
        gather_pass(h, 1, 1)
        gather_pass(h, 1, 2)

    def step4(h):
        for t in range(2):
            keys_add(h, t, 0)
            keys_add(h, t, 1)
            keys_add(h, t, 3)
        for t in range(2):
            keys_add(h, t, 2)
        keys_swap(h)

    step1(0)
    step2(0)
    step1(1)
    step3(0)
    hidden_wait()
    step2(1)
    step4(0)
    replicas_start()
    step3(1)
    deltas(0)
    arrived("delta", 0)
    scatter_far(0, 0)
    scatter_far(0, 1)
    step4(1)
    scatter_near(0, 0)
    scatter_near(0, 1)
    deltas(1)
    scatter_own(0, 0)
    first_far(0, 0)
    arrived("delta", 1)
    scatter_far(1, 0)
    scatter_far(1, 1)
    scatter_own(0, 1)
    first_far(0, 1)
    first_near(0, 0)
    scatter_near(1, 0)
    first_near(0, 1)
    scatter_near(1, 1)
    replicas_sum()
    first_own(0, 1)
    first_own(0, 0)
    scatter_own(1, 1)
    first_far(1, 1)
    scatter_own(1, 0)
    first_far(1, 0)
    first_near(1, 1)
    first_near(1, 0)
    finish(0)
    first_own(1, 1)
    first_own(1, 0)
    for k in (1, 2, 3):
        arrived("rep out", k)
    finish(1)
    for copy in sent.values():
        copy.wait_send()


def project(hidden, master, key_grad, diff):
    vmem = pl.BlockSpec(memory_space=pltpu.VMEM)
    f32, bf16 = jnp.float32, jnp.bfloat16
    return pl.pallas_call(
        kernel,
        out_shape=(
            jax.ShapeDtypeStruct((PARTS * WIDE, ROWS), f32),
            jax.ShapeDtypeStruct(diff.shape, f32),
        ),
        in_specs=[pl.BlockSpec(memory_space=pl.ANY), vmem, vmem, vmem],
        out_specs=(vmem, vmem),
        scratch_shapes=[
            pltpu.VMEM((2 * TOK, 32 * ROWS), bf16),
            pltpu.VMEM((PARTS, 32, ROWS, WIDE), bf16),
            pltpu.VMEM((PARTS, 2 * TOK, WIDE), f32),
            pltpu.VMEM((PARTS, TOK, WIDE), f32),
            pltpu.VMEM((PARTS, WIDE, 2 * TOK), bf16),
            pltpu.VMEM((PARTS, 2, 4, WIDE, 4 * ROWS), bf16),
            pltpu.VMEM((PARTS, 2, 4, WIDE, 4 * ROWS), bf16),
            pltpu.VMEM((PARTS, 2, WIDE, 4 * ROWS), f32),
            pltpu.VMEM((PARTS, WIDE, ROWS), f32),
            pltpu.VMEM((PARTS, WIDE, ROWS), f32),
            pltpu.VMEM((PARTS, WIDE, ROWS), f32),
            pltpu.VMEM((3, 256, 128), f32),
            pltpu.SemaphoreType.DMA((MESSAGES,)),
            pltpu.SemaphoreType.DMA((MESSAGES,)),
            pltpu.SemaphoreType.DMA((3,)),
        ],
        compiler_params=pltpu.CompilerParams(
            collective_id=0, has_side_effects=True, vmem_limit_bytes=56 * 2**20
        ),
        name="project",
    )(hidden, master, key_grad, diff)


def shards(
    hidden,
    master,
    moment_first,
    moment_second,
    key_grad,
    frag_global,
    frag_local,
    frag_moment,
    frag_index,
):
    weights = master[0]
    chosen = frag_index[0]
    glob = lax.dynamic_index_in_dim(frag_global, chosen, 0, keepdims=False)
    moment = lax.dynamic_index_in_dim(frag_moment, chosen, 0, keepdims=False)
    local = lax.dynamic_index_in_dim(frag_local[0], chosen, 0, keepdims=False)
    grad_t, delta = project(hidden[0], weights, key_grad[0], (glob - local).reshape(-1, 128))
    weights_new, first_new, second_new = adamw(weights, moment_first[0], moment_second[0], grad_t.T)
    delta = delta.reshape(-1)
    outer_moment = 0.9 * moment + delta
    outer_global = glob - 0.7 * (0.9 * outer_moment + delta)
    mixed_local = 0.5 * local + 0.5 * outer_global
    return (
        weights_new[None],
        first_new[None],
        second_new[None],
        outer_global,
        outer_moment,
        mixed_local[None],
    )


def solution(mesh):
    placed = (
        P("replica", "fsdp", None),
        P("replica", "fsdp", None),
        P("replica", "fsdp", None),
        P("replica", "fsdp", None),
        P("replica", "fsdp", None),
        P(None, "fsdp"),
        P("replica", None, "fsdp"),
        P(None, "fsdp"),
        P(),
    )
    return jax.shard_map(
        shards,
        mesh=mesh,
        in_specs=placed,
        out_specs=(
            P("replica", "fsdp", None),
            P("replica", "fsdp", None),
            P("replica", "fsdp", None),
            P("fsdp"),
            P("fsdp"),
            P("replica", "fsdp"),
        ),
        check_vma=False,
    )
```

time: 489 us -> 101 us (0.21)
  waiting for transfers between devices: 438 us -> 0 us
  Pallas kernels: 0 us -> 85.9 us
  matrix products: 17.9 us -> 0 us
  between operations: 16.3 us -> 1.53 us
    reduce_scatter x1 -> x0, waiting for transfers between devices: 307 us -> none  [shards(): lax.psum_scatter(jnp.dot(columns.T, key_delta, preferred_element_type=jnp...]
    all_gather x1 -> x0, waiting for transfers between devices: 131 us -> none  [shards(): lax.all_gather(weight_bf, 'fsdp', axis=0, tiled=True)]
    pallas_call x0 -> x1, Pallas kernels: none -> 85.9 us  [project(): pl.pallas_call(kernel, out_shape=(jax.ShapeDtypeStruct((PARTS * WIDE, ROW...]
    dot_general x2 -> x0, matrix products: 17.9 us -> none  [the longest x1 9.78 us: shards(): jnp.dot(columns, lax.all_gather(weight_bf, 'fsdp', axis=0, tiled=True), p...]
  transfers between devices with their start and end apart: 3 -> 0, of which waited for: 2 -> 0; matrix products, arithmetic and copies ran while one was open for 5% -> 0% of each run, Pallas kernels for 0% -> 0%
where the time goes in v1:
time: 101 us; the launch traced here: 99.9 us
  Pallas kernels  85.9 us (85%)
  other arithmetic  7.98 us (8%)
  local copies, waits for them, and re-layouts  4.55 us (5%)
  between operations  1.53 us (2%)
    pallas_call x1, Pallas kernels, project(): pl.pallas_call(kernel, out_shape=(jax.ShapeDtypeStruct((PARTS * WIDE, ROW...  85.9 us
    add x1, other arithmetic, shards(): mixed_local = 0.5 * local + 0.5 * outer_global  3.9 us
    sub x1, other arithmetic, shards(): outer_global = glob - 0.7 * (0.9 * outer_moment + delta)  2.15 us

profile of v1, /device:TPU:32, one launch (start us, length us, event | category | flops | bytes accessed | tf_op | source)
XLA Modules:
  0.0 99.9 jit_solution(9822066675679053494)
XLA Ops:
  0.6 0.0 copy-start.1
  0.6 0.0 copy-start.2
  1.5 0.0 copy-start.5
  1.5 1.8 %constant_dynamic-slice_fusion.1 = f32[1,131072]{1,0:T(1,128)S(1)} fusion(f32[2,131072]{1,0:T(2,128)} %param.14, s32[]{:T(128)S(6)} %select_n.6), kind=kLoop, calls=%fused_computation.15 | loop fusion | bytes 1048580 | tf_op jit(solution)/shard_map/jit(dynamic_index_in_dim)/dynamic_slice | solution.py:426
  3.2 1.7 %constant_dynamic-slice_fusion = f32[1,1,131072]{2,1,0:T(1,128)S(1)} fusion(f32[1,2,131072]{2,1,0:T(2,128)} %param.15, s32[]{:T(128)S(6)} %select_n.6), kind=kLoop, calls=%fused_computation.14 | loop fusion | bytes 1048580 | tf_op jit(solution)/shard_map/jit(dynamic_index_in_dim)/dynamic_slice | solution.py:428
  4.9 0.8 sub.13.diff
  5.8 0.0 copy-start
  5.8 0.0 copy-start.3
  5.8 0.0 copy-start.4
  5.8 85.9 %project.1 = (f32[512,128]{1,0:T(8,128)}, f32[1024,128]{1,0:T(8,128)}) custom-call(bf16[384,8192]{1,0:T(8,128)(2,1)} %bitcast.56, f32[128,512]{1,0:T(8,128)} %bitcast.62, bf16[384,512]{1,0:T(8,128)(2,1)} %bitcast.63, f32[1024,128]{1,0:T(8,128)} %sub.13.diff), custom_call_target="tpu_custom_call" | custom-call | tf_op jit(solution)/shard_map/project/pallas_call | solution.py:381
  91.7 0.0 copy-done.1
  91.7 0.0 copy-done.2
  91.7 0.0 copy-done.5
  91.7 3.9 %fusion = (f32[1,131072]{1,0:T(1,128)}, f32[1,131072]{1,0:T(1,128)S(1)}) fusion(f32[1,131072]{1,0:T(1,128)} %bitcast.60, f32[2,131072]{1,0:T(2,128)S(1)} %copy-done.5, s32[]{:T(128)S(6)} %select_n.6, f32[2,131072]{1,0:T(2,128)S(1)} %copy-done.1, f32[1,2,131072]{2,1,0:T(2,128)S(1)} %copy-done.2), kind=kLoop, calls=%fused_computation.1 | loop fusion | flops 1048576 | bytes 3145732 | tf_op jit(solution)/shard_map/add | solution.py:434
  95.6 2.2 %fusion.2 = (f32[131072]{0:T(1024)}, f32[131072]{0:T(1024)}) fusion(f32[131072]{0:T(1024)S(1)} %bitcast.58, f32[1024,128]{1,0:T(8,128)} %get-tuple-element.9, f32[131072]{0:T(1024)S(1)} %bitcast.61), kind=kLoop, calls=%fused_computation.5 | loop fusion | flops 655360 | bytes 2621440 | tf_op jit(solution)/shard_map/sub | solution.py:433
  97.8 1.1 %copy.15 = f32[512,128]{0,1:T(8,128)S(1)} copy(f32[512,128]{1,0:T(8,128)} %get-tuple-element.8) | data formatting | bytes 524288 | tf_op jit(solution)/shard_map/project/pallas_call | solution.py:381
  98.8 0.0 copy-done
  98.8 0.0 copy-done.3
  98.9 0.0 copy-done.4
  98.9 1.1 %fusion.6 = (f32[1,128,512]{2,1,0:T(8,128)}, f32[1,128,512]{2,1,0:T(8,128)}, f32[1,128,512]{2,1,0:T(8,128)}) fusion(f32[512,128]{0,1:T(8,128)S(1)} %copy.15, f32[1,128,512]{2,1,0:T(8,128)S(1)} %copy-done.3, f32[1,128,512]{2,1,0:T(8,128)S(1)} %copy-done.4, f32[1,128,512]{2,1,0:T(8,128)S(1)} %copy-done), kind=kLoop, calls=%fused_computation.13 | loop fusion | flops 983040 | bytes 1835008 | tf_op jit(solution)/shard_map/broadcast_in_dim | solution.py:438
Async XLA Ops:
  0.6 91.0 %copy-start.1 = (f32[2,131072]{1,0:T(2,128)S(1)}, f32[2,131072]{1,0:T(2,128)}, u32[]{:S(2)}) copy-start(f32[2,131072]{1,0:T(2,128)} %param.14) | copy-start | bytes 3145732
  0.6 91.0 %copy-start.2 = (f32[1,2,131072]{2,1,0:T(2,128)S(1)}, f32[1,2,131072]{2,1,0:T(2,128)}, u32[]{:S(2)}) copy-start(f32[1,2,131072]{2,1,0:T(2,128)} %param.15) | copy-start | bytes 3145732
  1.5 90.2 %copy-start.5 = (f32[2,131072]{1,0:T(2,128)S(1)}, f32[2,131072]{1,0:T(2,128)}, u32[]{:S(2)}) copy-start(f32[2,131072]{1,0:T(2,128)} %param.16) | copy-start | bytes 3145732
  5.8 93.1 %copy-start = (f32[1,128,512]{2,1,0:T(8,128)S(1)}, f32[1,128,512]{2,1,0:T(8,128)}, u32[]{:S(2)}) copy-start(f32[1,128,512]{2,1,0:T(8,128)} %param.10) | copy-start | bytes 786436
  5.8 93.1 %copy-start.3 = (f32[1,128,512]{2,1,0:T(8,128)S(1)}, f32[1,128,512]{2,1,0:T(8,128)}, u32[]{:S(2)}) copy-start(f32[1,128,512]{2,1,0:T(8,128)} %param.12) | copy-start | bytes 786436
  5.8 93.1 %copy-start.4 = (f32[1,128,512]{2,1,0:T(8,128)S(1)}, f32[1,128,512]{2,1,0:T(8,128)}, u32[]{:S(2)}) copy-start(f32[1,128,512]{2,1,0:T(8,128)} %param.11) | copy-start | bytes 786436

commit v2 on v0

v2 whole, which is shorter than its diff:
```python
import jax
import jax.numpy as jnp
from jax import lax
from jax.experimental import pallas as pl
from jax.experimental.pallas import tpu as pltpu
from jax.sharding import PartitionSpec as P

MESH = pl.DeviceIdType.MESH
HEAD = 128
PARTS = 2
WIDE = 256
TOK = 384
ROWS = 128
PAIR = 2 * ROWS
QUARTER = 256
MESSAGES = 256

ORDER = (
    ('zsend', 0),
    ('own', 0, 0),
    ('hids',),
    ('own', 1, 0),
    ('zsend', 1),
    ('own', 0, 1),
    ('passp', 0, 0, 0),
    ('passm', 0, 0, 0),
    ('nextm', 0, 0),
    ('rep',),
    ('passp', 1, 0, 0),
    ('passm', 1, 0, 0),
    ('nextp', 0, 0),
    ('passm', 0, 1, 0),
    ('passp', 0, 1, 0),
    ('hid',),
    ('nextp', 0, 1),
    ('nextm', 0, 1),
    ('passp', 0, 0, 1),
    ('passm', 0, 0, 1),
    ('far', 0, 0),
    ('keys', 0, 0, 0),
    ('own', 1, 1),
    ('passp', 0, 1, 3),
    ('passm', 0, 1, 3),
    ('far', 0, 1),
    ('keys', 0, 1, 0),
    ('passm', 0, 0, 3),
    ('passp', 0, 0, 3),
    ('passp', 0, 1, 1),
    ('passm', 0, 1, 1),
    ('passp', 0, 0, 2),
    ('passm', 0, 0, 2),
    ('keys', 0, 0, 1),
    ('keys', 0, 0, 3),
    ('passp', 1, 1, 0),
    ('passm', 1, 1, 0),
    ('nextp', 1, 0),
    ('nextm', 1, 0),
    ('rep2',),
    ('passp', 0, 1, 2),
    ('passm', 0, 1, 2),
    ('keys', 0, 1, 1),
    ('nextm', 1, 1),
    ('keys', 0, 1, 3),
    ('keys', 0, 0, 2),
    ('nextp', 1, 1),
    ('passp', 1, 0, 3),
    ('passm', 1, 0, 3),
    ('far', 1, 0),
    ('keys', 1, 0, 0),
    ('keys', 0, 1, 2),
    ('swap', 0),
    ('passp', 1, 0, 1),
    ('passm', 1, 0, 1),
    ('far', 1, 1),
    ('keys', 1, 1, 0),
    ('passp', 1, 1, 1),
    ('passm', 1, 1, 1),
    ('deltas', 0),
    ('passp', 1, 1, 3),
    ('passm', 1, 1, 3),
    ('passp', 1, 0, 2),
    ('keys', 1, 0, 3),
    ('passm', 1, 0, 2),
    ('keys', 1, 0, 1),
    ('rfar', 0, 1, 0),
    ('rfar', 0, 0, 0),
    ('passp', 1, 1, 2),
    ('passm', 1, 1, 2),
    ('keys', 1, 1, 1),
    ('keys', 1, 1, 3),
    ('rfar', 0, 1, 1),
    ('rfar', 0, 0, 1),
    ('row0', 0, 0, 0),
    ('row0', 0, 0, 1),
    ('keys', 1, 0, 2),
    ('rn1', 0, 1, 0),
    ('rn1', 0, 0, 0),
    ('rn3', 0, 1, 0),
    ('rn3', 0, 0, 0),
    ('rn1', 0, 0, 1),
    ('rn1b', 0, 1, 0),
    ('rn3b', 0, 0, 0),
    ('keys', 1, 1, 2),
    ('swap', 1),
    ('rn3b', 0, 1, 0),
    ('row0', 0, 1, 0),
    ('row0', 0, 1, 1),
    ('rn1b', 0, 0, 0),
    ('rn1', 0, 1, 1),
    ('rn3', 0, 1, 1),
    ('rn3', 0, 0, 1),
    ('deltas', 1),
    ('rn1b', 0, 1, 1),
    ('rn3b', 0, 0, 1),
    ('rn3b', 0, 1, 1),
    ('rn1b', 0, 0, 1),
    ('repf',),
    ('rfar', 1, 1, 0),
    ('rfar', 1, 0, 0),
    ('row', 0, 1, 0),
    ('row0', 1, 0, 0),
    ('row0', 1, 0, 1),
    ('row', 0, 0, 0),
    ('cn1', 0, 1),
    ('rfar', 1, 1, 1),
    ('rfar', 1, 0, 1),
    ('row0', 1, 1, 0),
    ('row0', 1, 1, 1),
    ('rn1', 1, 1, 0),
    ('rn3', 1, 1, 0),
    ('row', 0, 0, 1),
    ('row', 0, 1, 1),
    ('cfar', 0, 1),
    ('cn3', 0, 1),
    ('rn1', 1, 0, 0),
    ('rn1', 1, 1, 1),
    ('rn3', 1, 1, 1),
    ('rn3', 1, 0, 0),
    ('rn1', 1, 0, 1),
    ('rn1b', 1, 1, 0),
    ('rn3b', 1, 1, 0),
    ('rn3', 1, 0, 1),
    ('rn1b', 1, 0, 0),
    ('rn1b', 1, 1, 1),
    ('rn3b', 1, 1, 1),
    ('cn3b', 0, 1),
    ('rn3b', 1, 0, 0),
    ('cn1b', 0, 1),
    ('cn1', 0, 0),
    ('cn3', 0, 0),
    ('rn1b', 1, 0, 1),
    ('cfar', 0, 0),
    ('rn3b', 1, 0, 1),
    ('row', 1, 1, 0),
    ('cn1', 1, 1),
    ('row', 1, 1, 1),
    ('cfar', 1, 1),
    ('cn3', 1, 1),
    ('cown', 0, 1),
    ('row', 1, 0, 0),
    ('cn1', 1, 0),
    ('cn1b', 0, 0),
    ('cn3b', 0, 0),
    ('row', 1, 0, 1),
    ('cfar', 1, 0),
    ('cn3', 1, 0),
    ('cn3b', 1, 1),
    ('cn1b', 1, 1),
    ('cown', 0, 0),
    ('cn1b', 1, 0),
    ('cn3b', 1, 0),
    ('finish', 0),
    ('cown', 1, 1),
    ('cown', 1, 0),
    ('finish', 1),
)


def norm_backward(keys, upstream):
    inverse = lax.rsqrt(jnp.mean(keys * keys, axis=-1, keepdims=True) + 1e-06)
    normed = keys * inverse
    return inverse * (upstream - normed * jnp.mean(upstream * normed, axis=-1, keepdims=True))


def kernel(
    index,
    hidden,
    master_hbm,
    key_grad_hbm,
    glob_hbm,
    local_hbm,
    moment_hbm,
    grad_out,
    global_out,
    moment_out,
    mixed_out,
    hid,
    master,
    key_grad,
    wts,
    acc,
    acc_in,
    dlt,
    gbuf,
    stage,
    stage_in,
    z_stage,
    z_in,
    final,
    frags,
    diff,
    local,
    rep_in,
    delta,
    outer,
    send_sem,
    recv_sem,
    hid_sem,
    in_sem,
    out_sem,
):
    r = lax.axis_index("replica")
    f = lax.axis_index("fsdp")
    z, y, x, c = f // 32, (f // 8) % 4, (f // 2) % 4, f % 2

    def at(zz, yy, xx, cc):
        return (r, zz * 32 + (yy % 4) * 8 + (xx % 4) * 2 + cc)

    a_up, a_down = at(z, y + z, x + 1 - z, c), at(z, y + 4 - z, x + 3 + z, c)
    b_up, b_down = at(z, y + 1 - z, x + z, c), at(z, y + 3 + z, x + 4 - z, c)
    over_z, sibling = at(1 - z, y, x, c), at(z, y, x, 1 - c)
    reps = [((r + k) % 4, f) for k in (1, 2, 3)]
    ways = (((a_up, a_down), (b_up, b_down)), ((b_up, b_down), (a_up, a_down)))

    loads = [
        pltpu.make_async_copy(src, dst, in_sem.at[n])
        for n, (src, dst) in enumerate(
            (
                (master_hbm, master),
                (key_grad_hbm, key_grad),
                (glob_hbm, frags.at[0]),
                (local_hbm, frags.at[1]),
                (moment_hbm, frags.at[2]),
            )
        )
    ]
    loads[0].start()
    barrier = pltpu.get_barrier_semaphore()
    peers = [a_up, a_down, b_up, b_down, over_z, sibling, *reps]
    for peer in peers:
        pl.semaphore_signal(barrier, inc=1, device_id=peer, device_id_type=MESH)

    def chip_of(n):
        t, s, q = n // 16, (n // 4) % 4, n % 4
        plane = (z + t) % 2
        yy = (y + s * (1 - plane) + q * plane) % 4
        xx = (x + q * (1 - plane) + s * plane) % 4
        return plane * 16 + yy * 4 + xx

    def columns(block):
        return pl.ds(pl.multiple_of(block * ROWS, ROWS), ROWS)

    @pl.loop(0, 32)
    def _(n):
        pltpu.make_async_copy(
            hidden.at[:, columns(2 * chip_of(n) + c)], hid.at[pl.ds(0, TOK), columns(n)], hid_sem.at[0]
        ).start()

    for load in loads[1:]:
        load.start()
    loads[0].wait()
    wts[0, 0] = master[:, :WIDE].astype(jnp.bfloat16)
    wts[1, 0] = master[:, WIDE:].astype(jnp.bfloat16)
    pl.semaphore_wait(barrier, len(peers))

    sent = {}

    def send(name, src, dst, to):
        n = len(sent)
        copy = pltpu.make_async_remote_copy(
            src_ref=src,
            dst_ref=dst,
            send_sem=send_sem.at[n],
            recv_sem=recv_sem.at[n],
            device_id=to,
            device_id_type=MESH,
        )
        copy.start()
        sent[name] = copy

    def arrived(*name):
        sent[name].wait_recv()

    def slot(h, t, s, q):
        return wts.at[h, 16 * t + 4 * s + q]

    lower, upper = pl.ds(0, ROWS // 2), pl.ds(ROWS // 2, ROWS // 2)

    def zsend(h):
        send(("z", h), slot(h, 0, 0, 0), slot(h, 1, 0, 0), over_z)

    def over_second(h, t, q):
        _, (up, down) = ways[t]
        src = slot(h, t, 0, q)
        send(("s+", h, t, q), src, slot(h, t, 3, q), up)
        send(("s-", h, t, q), src, slot(h, t, 1, q), down)

    def own(h, t):
        (up, down), _ = ways[t]
        if t == 1:
            arrived("z", h)
        src = slot(h, t, 0, 0)
        send(("f+", h, t), src, slot(h, t, 0, 3), up)
        send(("f-", h, t), src, slot(h, t, 0, 1), down)
        over_second(h, t, 0)

    def nextp(h, t):
        arrived("f+", h, t)
        send(("ff+", h, t), slot(h, t, 0, 3).at[lower], slot(h, t, 0, 2).at[lower], ways[t][0][0])
        over_second(h, t, 3)

    def nextm(h, t):
        arrived("f-", h, t)
        send(("ff-", h, t), slot(h, t, 0, 1).at[upper], slot(h, t, 0, 2).at[upper], ways[t][0][1])
        over_second(h, t, 1)

    def far(h, t):
        arrived("ff+", h, t)
        arrived("ff-", h, t)
        over_second(h, t, 2)

    def passp(h, t, q):
        arrived("s+", h, t, q)
        send(("ss+", h, t, q), slot(h, t, 3, q).at[lower], slot(h, t, 2, q).at[lower], ways[t][1][0])

    def passm(h, t, q):
        arrived("s-", h, t, q)
        send(("ss-", h, t, q), slot(h, t, 1, q).at[upper], slot(h, t, 2, q).at[upper], ways[t][1][1])

    summed = set()

    def keys(h, t, s):
        if s == 2:
            for q in range(4):
                arrived("ss+", h, t, q)
                arrived("ss-", h, t, q)
        first = 16 * t + 4 * s
        part = jnp.dot(
            hid[:, first * ROWS : (first + 4) * ROWS],
            wts[h, first : first + 4].reshape(4 * ROWS, WIDE),
            preferred_element_type=jnp.float32,
        )
        if h in summed:
            acc[h] += part
        else:
            acc[h] = part
        summed.add(h)

    def swap(h):
        send(("keys", h), acc.at[h, pl.ds(TOK, TOK)], acc_in.at[h], sibling)

    def deltas(h):
        if h == 0:
            loads[1].wait()
        arrived("keys", h)
        for n in range(WIDE // HEAD):
            cols = slice(n * HEAD, (n + 1) * HEAD)
            of_head = acc[h, :TOK, cols] + acc_in[h, :, cols]
            at_col = h * WIDE + n * HEAD
            up = key_grad[:, at_col : at_col + HEAD].astype(jnp.float32)
            dlt[h, n * HEAD : (n + 1) * HEAD, :TOK] = norm_backward(of_head, up).T.astype(jnp.bfloat16)
        send(("delta", h), dlt.at[h, :, pl.ds(0, TOK)], dlt.at[h, :, pl.ds(TOK, TOK)], sibling)

    low, high, both = slice(0, WIDE // 2), slice(WIDE // 2, WIDE), slice(0, WIDE)
    swapped = set()

    def part_of(k):
        return slice(k * PAIR, (k + 1) * PAIR)

    def grad_row(h, t, s, k):
        if h not in swapped:
            arrived("delta", h)
            swapped.add(h)
        first = (16 * t + 4 * s + 2 * k) * ROWS
        return jnp.dot(dlt[h], hid[:, first : first + PAIR], preferred_element_type=jnp.float32)

    def row_send(name, h, t, s, k, rows, to):
        where = (h, t, s, pl.ds(rows.start, WIDE // 2), pl.ds(k * PAIR, PAIR))
        send((name, h, t, k), stage.at[where], stage_in.at[where], to)

    def one_send(name, h, t, q, rows, to):
        where = (h, t, 0, pl.ds(rows.start, WIDE // 2), pl.ds(q * ROWS, ROWS))
        send((name, h, t), stage.at[where], stage_in.at[where], to)

    def staged(h, t, s, rows, cols, value):
        stage[h, t, s, rows, cols] = value.astype(jnp.bfloat16)

    def received(h, t, s, rows, cols):
        return stage_in[h, t, s, rows, cols].astype(jnp.float32)

    def rfar(h, t, k):
        staged(h, t, 2, both, part_of(k), grad_row(h, t, 2, k))
        row_send("rf+", h, t, 2, k, low, ways[t][1][0])
        row_send("rf-", h, t, 2, k, high, ways[t][1][1])

    def rn1(h, t, k):
        cols = part_of(k)
        value = grad_row(h, t, 1, k)
        gbuf[h, t, 1, low, cols] = value[low]
        staged(h, t, 1, high, cols, value[high])
        row_send("r+h", h, t, 1, k, high, ways[t][1][0])

    def rn3(h, t, k):
        cols = part_of(k)
        value = grad_row(h, t, 3, k)
        gbuf[h, t, 3, high, cols] = value[high]
        staged(h, t, 3, low, cols, value[low])
        row_send("r-l", h, t, 3, k, low, ways[t][1][1])

    def rn1b(h, t, k):
        cols = part_of(k)
        arrived("rf+", h, t, k)
        staged(h, t, 1, low, cols, gbuf[h, t, 1, low, cols] + received(h, t, 2, low, cols))
        row_send("r+l", h, t, 1, k, low, ways[t][1][0])

    def rn3b(h, t, k):
        cols = part_of(k)
        arrived("rf-", h, t, k)
        staged(h, t, 3, high, cols, gbuf[h, t, 3, high, cols] + received(h, t, 2, high, cols))
        row_send("r-h", h, t, 3, k, high, ways[t][1][1])

    def row0(h, t, k):
        gbuf[h, t, 0, :, part_of(k)] = grad_row(h, t, 0, k)

    def row(h, t, k):
        for name in ("r+h", "r-l", "r+l", "r-h"):
            arrived(name, h, t, k)
        cols = part_of(k)
        gbuf[h, t, 0, :, cols] += received(h, t, 1, both, cols) + received(h, t, 3, both, cols)

    def cols_of(q):
        return slice(q * ROWS, (q + 1) * ROWS)

    def cfar(h, t):
        staged(h, t, 0, both, cols_of(2), gbuf[h, t, 0, :, cols_of(2)])
        one_send("cf+", h, t, 2, low, ways[t][0][0])
        one_send("cf-", h, t, 2, high, ways[t][0][1])

    def cn1(h, t):
        staged(h, t, 0, high, cols_of(1), gbuf[h, t, 0, high, cols_of(1)])
        one_send("c+h", h, t, 1, high, ways[t][0][0])

    def cn3(h, t):
        staged(h, t, 0, low, cols_of(3), gbuf[h, t, 0, low, cols_of(3)])
        one_send("c-l", h, t, 3, low, ways[t][0][1])

    def cn1b(h, t):
        arrived("cf+", h, t)
        staged(h, t, 0, low, cols_of(1), gbuf[h, t, 0, low, cols_of(1)] + received(h, t, 0, low, cols_of(2)))
        one_send("c+l", h, t, 1, low, ways[t][0][0])

    def cn3b(h, t):
        arrived("cf-", h, t)
        staged(h, t, 0, high, cols_of(3), gbuf[h, t, 0, high, cols_of(3)] + received(h, t, 0, high, cols_of(2)))
        one_send("c-h", h, t, 3, high, ways[t][0][1])

    def cown(h, t):
        for name in ("c+h", "c-l", "c+l", "c-h"):
            arrived(name, h, t)
        total = gbuf[h, t, 0, :, cols_of(0)] + received(h, t, 0, both, cols_of(1)) + received(h, t, 0, both, cols_of(3))
        if t == 1:
            z_stage[h] = total
            send(("gz", h), z_stage.at[h], z_in.at[h], over_z)
        else:
            final[h] = total

    def finish(h):
        arrived("gz", h)
        grad_out[:, h * WIDE : (h + 1) * WIDE] = (final[h] + z_in[h]).T

    def hids():
        @pl.loop(0, 32)
        def _(n):
            pltpu.make_async_remote_copy(
                src_ref=hidden.at[:, columns(2 * chip_of(n) + 1 - c)],
                dst_ref=hid.at[pl.ds(TOK, TOK), columns(n)],
                send_sem=hid_sem.at[1],
                recv_sem=hid_sem.at[2],
                device_id=sibling,
                device_id_type=MESH,
            ).start()

    mine, theirs = hid.at[pl.ds(0, TOK)], hid.at[pl.ds(TOK, TOK)]

    def hid_wait():
        pltpu.make_async_copy(mine, mine, hid_sem.at[0]).wait()
        pltpu.make_async_copy(theirs, theirs, hid_sem.at[2]).wait()

    def chosen(n, rows):
        first = frags[n, pl.ds(2 * rows.start, rows.size, stride=2), :]
        second = frags[n, pl.ds(2 * rows.start + 1, rows.size, stride=2), :]
        return jnp.where(index[0] == 0, first, second)

    def rep():
        loads[2].wait()
        loads[3].wait()
        for n in range(4):
            rows = pl.ds(n * QUARTER, QUARTER)
            own_local = chosen(1, rows)
            local[rows, :] = own_local
            diff[rows, :] = chosen(0, rows) - own_local
        for k, to in zip((1, 2, 3), reps):
            send(("rep", k), diff.at[pl.ds(((r + k) % 4) * QUARTER, QUARTER)], rep_in.at[k - 1], to)

    def rep2():
        for k in (1, 2, 3):
            arrived("rep", k)
        own_rows = pl.ds(r * QUARTER, QUARTER)
        delta[own_rows, :] = (diff[own_rows, :] + rep_in[0] + rep_in[1] + rep_in[2]) * 0.25
        for k, to in zip((1, 2, 3), reps):
            send(("rep out", k), delta.at[own_rows], delta.at[own_rows], to)

    stores = [
        pltpu.make_async_copy(outer.at[n], dst, out_sem.at[n])
        for n, dst in enumerate((global_out, moment_out, mixed_out))
    ]

    def repf():
        loads[4].wait()
        for k in (1, 2, 3):
            arrived("rep out", k)
        for n in range(4):
            rows = pl.ds(n * QUARTER, QUARTER)
            step = delta[rows, :]
            outer_moment = 0.9 * chosen(2, rows) + step
            outer_global = chosen(0, rows) - 0.7 * (0.9 * outer_moment + step)
            outer[0, rows, :] = outer_global
            outer[1, rows, :] = outer_moment
            outer[2, rows, :] = 0.5 * local[rows, :] + 0.5 * outer_global
        for store in stores:
            store.start()

    steps = dict(
        zsend=zsend, own=own, nextp=nextp, nextm=nextm, far=far, passp=passp, passm=passm, keys=keys, swap=swap,
        deltas=deltas, rfar=rfar, rn1=rn1, rn3=rn3, rn1b=rn1b, rn3b=rn3b, row0=row0, row=row, cfar=cfar, cn1=cn1,
        cn3=cn3, cn1b=cn1b, cn3b=cn3b, cown=cown, finish=finish, hids=hids, hid=hid_wait, rep=rep, rep2=rep2, repf=repf,
    )
    for name, *where in ORDER:
        steps[name](*where)
    for copy in sent.values():
        copy.wait_send()
    pltpu.make_async_copy(mine, mine, hid_sem.at[1]).wait()
    for store in stores:
        store.wait()


def project(index, hidden, master, key_grad, glob, local, moment):
    vmem, anywhere = pl.BlockSpec(memory_space=pltpu.VMEM), pl.BlockSpec(memory_space=pl.ANY)
    f32, bf16 = jnp.float32, jnp.bfloat16
    part = (4 * QUARTER, 128)
    row = (PARTS, 2, 4, WIDE, 4 * ROWS)
    return pl.pallas_call(
        kernel,
        out_shape=(
            jax.ShapeDtypeStruct((ROWS, PARTS * WIDE), f32),
            *[jax.ShapeDtypeStruct(part, f32)] * 3,
        ),
        in_specs=[pl.BlockSpec(memory_space=pltpu.SMEM), *[anywhere] * 6],
        out_specs=(vmem, *[anywhere] * 3),
        scratch_shapes=[
            pltpu.VMEM((2 * TOK, 32 * ROWS), bf16),
            pltpu.VMEM((ROWS, PARTS * WIDE), f32),
            pltpu.VMEM((TOK, PARTS * WIDE), bf16),
            pltpu.VMEM((PARTS, 32, ROWS, WIDE), bf16),
            pltpu.VMEM((PARTS, 2 * TOK, WIDE), f32),
            pltpu.VMEM((PARTS, TOK, WIDE), f32),
            pltpu.VMEM((PARTS, WIDE, 2 * TOK), bf16),
            pltpu.VMEM(row, f32),
            pltpu.VMEM(row, bf16),
            pltpu.VMEM(row, bf16),
            pltpu.VMEM((PARTS, WIDE, ROWS), f32),
            pltpu.VMEM((PARTS, WIDE, ROWS), f32),
            pltpu.VMEM((PARTS, WIDE, ROWS), f32),
            pltpu.VMEM((3, 8 * QUARTER, 128), f32),
            pltpu.VMEM(part, f32),
            pltpu.VMEM(part, f32),
            pltpu.VMEM((3, QUARTER, 128), f32),
            pltpu.VMEM(part, f32),
            pltpu.VMEM((3, *part), f32),
            pltpu.SemaphoreType.DMA((MESSAGES,)),
            pltpu.SemaphoreType.DMA((MESSAGES,)),
            pltpu.SemaphoreType.DMA((3,)),
            pltpu.SemaphoreType.DMA((5,)),
            pltpu.SemaphoreType.DMA((3,)),
        ],
        compiler_params=pltpu.CompilerParams(
            collective_id=0, has_side_effects=True, vmem_limit_bytes=56 * 2**20
        ),
        name="project",
    )(index, hidden, master, key_grad, glob, local, moment)


def last_kernel(*refs):
    ins, outs, states, outer, in_sem, out_sem = refs[:7], refs[7:13], *refs[13:]
    held = [states.at[n] for n in range(4)] + [outer.at[n] for n in range(3)]
    results = [states.at[n] for n in range(4, 7)] + [outer.at[n] for n in range(3)]
    loads = [pltpu.make_async_copy(src, dst, in_sem.at[n]) for n, (src, dst) in enumerate(zip(ins, held))]
    stores = [pltpu.make_async_copy(src, dst, out_sem.at[n]) for n, (src, dst) in enumerate(zip(results, outs))]
    for load in loads:
        load.start()
    for load in loads[:4]:
        load.wait()
    gradient, weights = states[0], states[1]
    first_new = 0.9 * states[2] + 0.1 * gradient
    second_new = 0.95 * states[3] + 0.05 * gradient * gradient
    first_hat = first_new / (1.0 - 0.9**10)
    second_hat = second_new / (1.0 - 0.95**10)
    states[4] = weights - 0.01 * (first_hat / (jnp.sqrt(second_hat) + 1e-08) + 0.1 * weights)
    states[5] = first_new
    states[6] = second_new
    for store in stores[:3]:
        store.start()
    for load, store in zip(loads[4:], stores[3:]):
        load.wait()
        store.start()
    for store in stores:
        store.wait()


def last(grad, master, first, second, *outer):
    anywhere = pl.BlockSpec(memory_space=pl.ANY)
    return pl.pallas_call(
        last_kernel,
        out_shape=tuple(jax.ShapeDtypeStruct(v.shape, jnp.float32) for v in (master, first, second, *outer)),
        in_specs=[anywhere] * 7,
        out_specs=(anywhere,) * 6,
        scratch_shapes=[
            pltpu.VMEM((7, *master.shape), jnp.float32),
            pltpu.VMEM((3, *outer[0].shape), jnp.float32),
            pltpu.SemaphoreType.DMA((7,)),
            pltpu.SemaphoreType.DMA((6,)),
        ],
        compiler_params=pltpu.CompilerParams(vmem_limit_bytes=56 * 2**20),
        name="last",
    )(grad, master, first, second, *outer)


def rows_of(fragments):
    return fragments.reshape(2, -1, 128).transpose(1, 0, 2).reshape(-1, 128)


def shards(
    hidden,
    master,
    moment_first,
    moment_second,
    key_grad,
    frag_global,
    frag_local,
    frag_moment,
    frag_index,
):
    grad, *outer = project(
        frag_index,
        hidden[0],
        master[0],
        key_grad[0],
        rows_of(frag_global),
        rows_of(frag_local[0]),
        rows_of(frag_moment),
    )
    weights_new, first_new, second_new, *outer = last(grad, master[0], moment_first[0], moment_second[0], *outer)
    outer_global, outer_moment, mixed_local = (part.reshape(-1) for part in outer)
    return (
        weights_new[None],
        first_new[None],
        second_new[None],
        outer_global,
        outer_moment,
        mixed_local[None],
    )


def solution(mesh):
    placed = (
        P("replica", "fsdp", None),
        P("replica", "fsdp", None),
        P("replica", "fsdp", None),
        P("replica", "fsdp", None),
        P("replica", "fsdp", None),
        P(None, "fsdp"),
        P("replica", None, "fsdp"),
        P(None, "fsdp"),
        P(),
    )
    return jax.shard_map(
        shards,
        mesh=mesh,
        in_specs=placed,
        out_specs=(
            P("replica", "fsdp", None),
            P("replica", "fsdp", None),
            P("replica", "fsdp", None),
            P("fsdp"),
            P("fsdp"),
            P("replica", "fsdp"),
        ),
        check_vma=False,
    )
```

time: 489 us -> 78.3 us (0.16)
  waiting for transfers between devices: 438 us -> 0 us
  Pallas kernels: 0 us -> 76.9 us
  matrix products: 17.9 us -> 0 us
  between operations: 16.3 us -> 1.29 us
  local copies, waits for them, and re-layouts: 8.14 us -> 0 us
  other arithmetic: 7.2 us -> 0 us
    reduce_scatter x1 -> x0, waiting for transfers between devices: 307 us -> none  [shards(): lax.psum_scatter(jnp.dot(columns.T, key_delta, preferred_element_type=jnp...]
    all_gather x1 -> x0, waiting for transfers between devices: 131 us -> none  [shards(): lax.all_gather(weight_bf, 'fsdp', axis=0, tiled=True)]
    pallas_call x0 -> x2, Pallas kernels: none -> 76.9 us  [the longest x1 74 us: project(): pl.pallas_call(kernel, out_shape=(jax.ShapeDtypeStruct((ROWS, PARTS * WID...]
    dot_general x2 -> x0, matrix products: 17.9 us -> none  [the longest x1 9.78 us: shards(): jnp.dot(columns, lax.all_gather(weight_bf, 'fsdp', axis=0, tiled=True), p...]
  transfers between devices with their start and end apart: 3 -> 0, of which waited for: 2 -> 0; matrix products, arithmetic and copies ran while one was open for 5% -> 0% of each run, Pallas kernels for 0% -> 0%
where the time goes in v2:
time: 78.3 us; the launch traced here: 78.2 us
  Pallas kernels  76.9 us (98%)
  between operations  1.29 us (2%)
    pallas_call x1, Pallas kernels, project(): pl.pallas_call(kernel, out_shape=(jax.ShapeDtypeStruct((ROWS, PARTS * WID...  74 us
    pallas_call x1, Pallas kernels, last(): pl.pallas_call(last_kernel, out_shape=tuple((jax.ShapeDtypeStruct(v.shape...  2.91 us

profile of v2, /device:TPU:32, one launch (start us, length us, event | category | flops | bytes accessed | tf_op | source)
XLA Modules:
  0.0 78.2 jit_solution(1983353551140974354)
XLA Ops:
  1.3 74.0 %project.1 = (f32[128,512]{1,0:T(8,128)}, f32[1024,128]{1,0:T(8,128)}, f32[1024,128]{1,0:T(8,128)}, f32[1024,128]{1,0:T(8,128)}) custom-call(s32[1]{0:T(128)S(6)} %copy.18.index, bf16[384,8192]{1,0:T(8,128)(2,1)} %bitcast.26, f32[128,512]{1,0:T(8,128)} %bitcast.30, bf16[384,512]{1,0:T(8,128)(2,1)} %bitcast.32, f32[2048,128]{1,0:T(8,128)} %bitcast.27, ...), custom_call_target="tpu_custom_call" | custom-call | tf_op jit(solution)/shard_map/project/pallas_call | solution.py:562
  75.3 2.9 %last.1 = (f32[128,512]{1,0:T(8,128)}, f32[128,512]{1,0:T(8,128)}, f32[128,512]{1,0:T(8,128)}, f32[1024,128]{1,0:T(8,128)}, f32[1024,128]{1,0:T(8,128)}, /*index=5*/f32[1024,128]{1,0:T(8,128)}) custom-call(f32[128,512]{1,0:T(8,128)} %get-tuple-element.16.refs_0_, f32[128,512]{1,0:T(8,128)} %bitcast.31, f32[128,512]{1,0:T(8,128)} %bitcast.33, ...), custom_call_target="tpu_custom_call" | custom-call | tf_op jit(solution)/shard_map/last/pallas_call | solution.py:632

commit v3 on v2

v3 whole, which is shorter than its diff:
```python
import jax
import jax.numpy as jnp
from jax import lax
from jax.experimental import pallas as pl
from jax.experimental.pallas import tpu as pltpu
from jax.sharding import PartitionSpec as P

MESH = pl.DeviceIdType.MESH
HEAD = 128
PARTS = 2
WIDE = 256
TOK = 384
ROWS = 128
SLOTS = 1
QUARTER = 256
ARRIVALS = 120

ORDER = (
    ('zsend', 0),
    ('own', 1, 0),
    ('hids',),
    ('zsend', 1),
    ('own', 0, 0),
    ('own', 0, 1),
    ('passp', 1, 0, 0),
    ('passm', 1, 0, 0),
    ('nextm', 1, 0),
    ('rep',),
    ('passm', 0, 0, 0),
    ('passp', 0, 0, 0),
    ('nextp', 0, 0),
    ('nextm', 0, 0),
    ('passp', 0, 1, 0),
    ('passm', 0, 1, 0),
    ('hid',),
    ('kgt',),
    ('nextm', 0, 1),
    ('nextp', 0, 1),
    ('passm', 0, 0, 3),
    ('passp', 0, 0, 3),
    ('far', 0, 0),
    ('passp', 1, 0, 1),
    ('passm', 1, 0, 1),
    ('own', 1, 1),
    ('passp', 0, 1, 1),
    ('passm', 0, 1, 1),
    ('passm', 0, 0, 1),
    ('passp', 0, 0, 1),
    ('far', 0, 1),
    ('keys', 0, 0),
    ('passp', 0, 1, 3),
    ('passm', 0, 1, 3),
    ('passm', 0, 0, 2),
    ('passp', 0, 0, 2),
    ('keys', 0, 1),
    ('nextp', 1, 0),
    ('passm', 1, 1, 0),
    ('passp', 1, 1, 0),
    ('nextp', 1, 1),
    ('nextm', 1, 1),
    ('keys', 0, 3),
    ('passm', 0, 1, 2),
    ('passp', 0, 1, 2),
    ('keys', 0, 2),
    ('far', 1, 0),
    ('passp', 1, 0, 3),
    ('passm', 1, 0, 3),
    ('passm', 1, 1, 3),
    ('passp', 1, 1, 3),
    ('far', 1, 1),
    ('keys', 1, 0),
    ('keys', 0, 4),
    ('passm', 1, 1, 1),
    ('swap', 0),
    ('passp', 1, 1, 1),
    ('rep2',),
    ('passp', 1, 0, 2),
    ('passm', 1, 0, 2),
    ('keys', 1, 1),
    ('deltas', 0),
    ('passm', 1, 1, 2),
    ('passp', 1, 1, 2),
    ('keys', 1, 2),
    ('grad', 0, 2),
    ('rfar', 0, 0, 2),
    ('rfar', 0, 1, 3),
    ('rfar', 0, 1, 1),
    ('rfar', 0, 0, 0),
    ('keys', 1, 3),
    ('rfar', 0, 1, 0),
    ('rfar', 0, 0, 3),
    ('grad', 0, 0),
    ('rfar', 0, 1, 2),
    ('rfar', 0, 0, 1),
    ('keys', 1, 4),
    ('swap', 1),
    ('grad', 0, 3),
    ('rn3', 0, 0, 3),
    ('rn3', 0, 0, 0),
    ('rn3', 0, 1, 3),
    ('rn3', 0, 1, 2),
    ('grad', 0, 1),
    ('rn1', 0, 1, 2),
    ('rn1', 0, 1, 1),
    ('rn1', 0, 0, 2),
    ('rn1b', 0, 0, 2),
    ('rn3', 0, 0, 2),
    ('rn3', 0, 1, 1),
    ('rn3b', 0, 0, 2),
    ('rn1b', 0, 1, 1),
    ('deltas', 1),
    ('rn1', 0, 0, 1),
    ('rn3b', 0, 1, 1),
    ('rn3', 0, 0, 1),
    ('rn3b', 0, 1, 3),
    ('rn1', 0, 1, 0),
    ('rn1', 0, 0, 3),
    ('rn3b', 0, 0, 3),
    ('rn1b', 0, 1, 2),
    ('rn1b', 0, 0, 3),
    ('rn3b', 0, 1, 2),
    ('grad', 1, 2),
    ('rfar', 1, 0, 1),
    ('rfar', 1, 1, 2),
    ('grad', 1, 3),
    ('rfar', 1, 1, 1),
    ('rn1', 0, 1, 3),
    ('rn1b', 0, 1, 3),
    ('rfar', 1, 1, 3),
    ('rn3', 1, 0, 1),
    ('rn3', 1, 0, 2),
    ('grad', 1, 1),
    ('row', 0, 0, 2),
    ('rn1', 1, 0, 2),
    ('row', 0, 1, 1),
    ('rn1', 1, 1, 3),
    ('rn3', 1, 1, 2),
    ('rn3', 1, 1, 3),
    ('rfar', 1, 0, 2),
    ('rn1', 1, 1, 2),
    ('rn3', 1, 0, 0),
    ('grad', 1, 0),
    ('row', 0, 0, 3),
    ('row', 0, 1, 2),
    ('rn1b', 0, 1, 0),
    ('rn3b', 1, 1, 2),
    ('rn1b', 1, 1, 2),
    ('rn3b', 1, 0, 1),
    ('rn1', 1, 0, 1),
    ('rn1', 1, 1, 1),
    ('rn3', 1, 1, 1),
    ('rn3', 1, 0, 3),
    ('rn3b', 1, 1, 1),
    ('rn1b', 1, 0, 1),
    ('rn1b', 1, 1, 1),
    ('rn3', 0, 1, 0),
    ('row', 0, 1, 3),
    ('rn3b', 1, 1, 3),
    ('rn1b', 1, 1, 3),
    ('rfar', 1, 0, 3),
    ('repf',),
    ('rn3b', 1, 0, 2),
    ('rn1b', 1, 0, 2),
    ('rn1b', 0, 0, 1),
    ('rn1', 1, 0, 0),
    ('rfar', 1, 1, 0),
    ('rn3', 1, 1, 0),
    ('rn3b', 0, 1, 0),
    ('row', 1, 1, 2),
    ('zadd', 0, 2),
    ('rn1', 0, 0, 0),
    ('rn1', 1, 0, 3),
    ('rn3b', 0, 0, 1),
    ('rn3b', 0, 0, 0),
    ('rn1b', 0, 0, 0),
    ('cfar', 0),
    ('row', 1, 0, 1),
    ('row', 1, 1, 1),
    ('rn1', 1, 1, 0),
    ('rfar', 1, 0, 0),
    ('zadd', 0, 3),
    ('cn3', 0),
    ('row', 1, 1, 3),
    ('rn1b', 1, 0, 3),
    ('rn3b', 1, 0, 3),
    ('rn3b', 1, 1, 0),
    ('row', 1, 0, 2),
    ('row', 0, 1, 0),
    ('rn1b', 1, 1, 0),
    ('zadd', 1, 2),
    ('cfar', 1),
    ('row', 0, 0, 1),
    ('zadd', 0, 1),
    ('cn1', 0),
    ('cn3b', 0),
    ('cn1b', 0),
    ('row', 0, 0, 0),
    ('rn3b', 1, 0, 0),
    ('zadd', 1, 1),
    ('cn1', 1),
    ('rn1b', 1, 0, 0),
    ('row', 1, 0, 3),
    ('zadd', 1, 3),
    ('row', 1, 1, 0),
    ('cn3', 1),
    ('cn3b', 1),
    ('cn1b', 1),
    ('zadd', 0, 0),
    ('finish', 0),
    ('row', 1, 0, 0),
    ('zadd', 1, 0),
    ('finish', 1),
)


def norm_backward(keys, upstream):
    inverse = lax.rsqrt(jnp.mean(keys * keys, axis=0, keepdims=True) + 1e-06)
    normed = keys * inverse
    return inverse * (upstream - normed * jnp.mean(upstream * normed, axis=0, keepdims=True))


def kernel(
    index,
    hidden,
    master_hbm,
    key_grad_hbm,
    glob_hbm,
    local_hbm,
    moment_hbm,
    grad_out,
    global_out,
    moment_out,
    mixed_out,
    hid,
    master,
    key_grad,
    key_grad_t,
    wts,
    acc,
    acc_in,
    dlt,
    gbuf,
    stage,
    stage_in,
    z_stage,
    z_in,
    wide,
    wide_in,
    frags,
    diff,
    local,
    rep_in,
    delta,
    outer,
    send_sem,
    recv_sem,
    hid_sem,
    in_sem,
    out_sem,
):
    r = lax.axis_index("replica")
    f = lax.axis_index("fsdp")
    z, y, x, c = f // 32, (f // 8) % 4, (f // 2) % 4, f % 2

    def at(zz, yy, xx, cc):
        return (r, zz * 32 + (yy % 4) * 8 + (xx % 4) * 2 + cc)

    a_up, a_down = at(z, y + z, x + 1 - z, c), at(z, y + 4 - z, x + 3 + z, c)
    b_up, b_down = at(z, y + 1 - z, x + z, c), at(z, y + 3 + z, x + 4 - z, c)
    over_z, sibling = at(1 - z, y, x, c), at(z, y, x, 1 - c)
    reps = [((r + k) % 4, f) for k in (1, 2, 3)]
    axes = ((a_up, a_down), (b_up, b_down))

    def ways(h, t):
        return axes if (h + t) % 2 == 0 else axes[::-1]


    loads = [
        pltpu.make_async_copy(src, dst, in_sem.at[n])
        for n, (src, dst) in enumerate(
            (
                (master_hbm, master),
                (key_grad_hbm, key_grad),
                (glob_hbm, frags.at[0]),
                (local_hbm, frags.at[1]),
                (moment_hbm, frags.at[2]),
            )
        )
    ]
    loads[0].start()
    barrier = pltpu.get_barrier_semaphore()
    peers = [a_up, a_down, b_up, b_down, over_z, sibling, *reps]
    for peer in peers:
        pl.semaphore_signal(barrier, inc=1, device_id=peer, device_id_type=MESH)

    def chip_of(n):
        t, s, q = n // 16, (n // 4) % 4, n % 4
        plane = (z + t) % 2
        yy = (y + s * (1 - plane) + q * plane) % 4
        xx = (x + q * (1 - plane) + s * plane) % 4
        return plane * 16 + yy * 4 + xx

    def columns(block):
        return pl.ds(pl.multiple_of(block * ROWS, ROWS), ROWS)

    @pl.loop(0, 32)
    def _(n):
        pltpu.make_async_copy(
            hidden.at[:, columns(2 * chip_of(n) + c)], hid.at[pl.ds(0, TOK), columns(n)], hid_sem.at[0]
        ).start()

    for load in loads[1:]:
        load.start()
    loads[0].wait()
    wts[0, 0] = master[:, :WIDE].T.astype(jnp.bfloat16)
    wts[1, 0] = master[:, WIDE:].T.astype(jnp.bfloat16)
    pl.semaphore_wait(barrier, len(peers))

    arrivals = {}

    def send(what, group, src, dst, to):
        pltpu.make_async_remote_copy(
            src_ref=src,
            dst_ref=dst,
            send_sem=send_sem.at[group],
            recv_sem=recv_sem.at[arrivals.setdefault(what, len(arrivals))],
            device_id=to,
            device_id_type=MESH,
        ).start()

    def taken(semaphore, as_large):
        pltpu.make_async_copy(as_large, as_large, semaphore).wait()

    def arrived(what, as_large):
        taken(recv_sem.at[arrivals[what]], as_large)

    gather, scatter, sums, keys_swap, delta_swap, summed, spread = range(7)

    def slot(h, t, s, q):
        return wts.at[h, 16 * t + 4 * s + q]

    lower, upper = pl.ds(0, WIDE // 2), pl.ds(WIDE // 2, WIDE // 2)

    def zsend(h):
        send(("z", h), gather, slot(h, 0, 0, 0), slot(h, 1, 0, 0), over_z)

    def over_second(h, t, q):
        _, (up, down) = ways(h, t)
        src = slot(h, t, 0, q)
        send(("s+", h, t, q), gather, src, slot(h, t, 3, q), up)
        send(("s-", h, t, q), gather, src, slot(h, t, 1, q), down)

    def own(h, t):
        (up, down), _ = ways(h, t)
        if t == 1:
            arrived(("z", h), slot(h, 1, 0, 0))
        src = slot(h, t, 0, 0)
        send(("f+", h, t), gather, src, slot(h, t, 0, 3), up)
        send(("f-", h, t), gather, src, slot(h, t, 0, 1), down)
        over_second(h, t, 0)

    def nextp(h, t):
        arrived(("f+", h, t), slot(h, t, 0, 3))
        send(("ff", h, t), gather, slot(h, t, 0, 3).at[lower], slot(h, t, 0, 2).at[lower], ways(h, t)[0][0])
        over_second(h, t, 3)

    def nextm(h, t):
        arrived(("f-", h, t), slot(h, t, 0, 1))
        send(("ff", h, t), gather, slot(h, t, 0, 1).at[upper], slot(h, t, 0, 2).at[upper], ways(h, t)[0][1])
        over_second(h, t, 1)

    def far(h, t):
        arrived(("ff", h, t), slot(h, t, 0, 2))
        over_second(h, t, 2)

    def passp(h, t, q):
        arrived(("s+", h, t, q), slot(h, t, 3, q))
        send(("ss", h, t), gather, slot(h, t, 3, q).at[lower], slot(h, t, 2, q).at[lower], ways(h, t)[1][0])

    def passm(h, t, q):
        arrived(("s-", h, t, q), slot(h, t, 1, q))
        send(("ss", h, t), gather, slot(h, t, 1, q).at[upper], slot(h, t, 2, q).at[upper], ways(h, t)[1][1])

    def hidden_of(h, rows):
        blocks = [16 * t + (4 * s + q if h == 0 else 4 * q + s) for t, s in rows for q in range(4)]
        return jnp.concatenate([hid[:, n * ROWS : (n + 1) * ROWS] for n in blocks], axis=1)

    def keys(h, n):
        rows = (((0, 0), (1, 0)), ((0, 1), (0, 3)), ((1, 1), (1, 3)), ((0, 2),), ((1, 2),))[n]
        if n >= 3:
            arrived(("ss", h, n - 3), wts.at[h, pl.ds(0, 4)])
        weights = [wts[h, 16 * t + 4 * s + q] for t, s in rows for q in range(4)]
        part = lax.dot_general(
            jnp.concatenate(weights, axis=1),
            hidden_of(h, rows),
            (((1,), (1,)), ((), ())),
            preferred_element_type=jnp.float32,
        )
        if n == 0:
            acc[h] = part
        else:
            acc[h] += part

    def swap(h):
        send(("keys", h), keys_swap, acc.at[h, :, pl.ds(TOK, TOK)], acc_in.at[h], sibling)

    def kgt():
        loads[1].wait()
        key_grad_t[...] = key_grad[...].astype(jnp.float32).T

    def deltas(h):
        arrived(("keys", h), acc_in.at[h])
        for n in range(WIDE // HEAD):
            rows, of_all = pl.ds(n * HEAD, HEAD), pl.ds(h * WIDE + n * HEAD, HEAD)
            of_head = acc[h, rows, :TOK] + acc_in[h, rows, :]
            dlt[h, rows, :TOK] = norm_backward(of_head, key_grad_t[of_all, :]).astype(jnp.bfloat16)
        send(("delta", h), delta_swap, dlt.at[h, :, pl.ds(0, TOK)], dlt.at[h, :, pl.ds(TOK, TOK)], sibling)

    low, high, both = slice(0, WIDE // 2), slice(WIDE // 2, WIDE), slice(0, WIDE)

    def grad(h, s):
        if s == 2:
            arrived(("delta", h), dlt.at[h, :, pl.ds(TOK, TOK)])
        value = jnp.dot(dlt[h], hidden_of(h, ((0, s), (1, s))), preferred_element_type=jnp.float32)
        for t in range(2):
            one = value[:, t * 4 * ROWS : (t + 1) * 4 * ROWS]
            if s == 2:
                stage[h, t, s] = one.astype(jnp.bfloat16)
            elif s == 0:
                gbuf[h, t, s] = one
            else:
                now, later = (high, low) if s == 1 else (low, high)
                stage[h, t, s, now, :] = one[now].astype(jnp.bfloat16)
                gbuf[h, t, s, later, :] = one[later]

    def cols_of(q):
        return slice(q * ROWS, (q + 1) * ROWS)

    def cols_in(k):
        return slice(k * SLOTS * ROWS, (k + 1) * SLOTS * ROWS)

    def half_of(h, t, s, k, rows):
        return (h, t, s, pl.ds(rows.start, WIDE // 2), pl.ds(k * SLOTS * ROWS, SLOTS * ROWS))

    def row_send(name, h, t, s, k, rows, to):
        where = half_of(h, t, s, k, rows)
        send((name, h, t, k), scatter, stage.at[where], stage_in.at[where], to)

    def received(h, t, s, cols, rows):
        return stage_in[h, t, s, rows, cols].astype(jnp.float32)

    def rfar(h, t, k):
        row_send("rf+", h, t, 2, k, low, ways(h, t)[1][0])
        row_send("rf-", h, t, 2, k, high, ways(h, t)[1][1])

    def rn1(h, t, k):
        row_send("r", h, t, 1, k, high, ways(h, t)[1][0])

    def rn3(h, t, k):
        row_send("r", h, t, 3, k, low, ways(h, t)[1][1])

    def rn1b(h, t, k):
        arrived(("rf+", h, t, k), stage_in.at[half_of(h, t, 2, k, low)])
        total = gbuf[h, t, 1, low, cols_in(k)] + received(h, t, 2, cols_in(k), low)
        stage[h, t, 1, low, cols_in(k)] = total.astype(jnp.bfloat16)
        row_send("r", h, t, 1, k, low, ways(h, t)[1][0])

    def rn3b(h, t, k):
        arrived(("rf-", h, t, k), stage_in.at[half_of(h, t, 2, k, high)])
        total = gbuf[h, t, 3, high, cols_in(k)] + received(h, t, 2, cols_in(k), high)
        stage[h, t, 3, high, cols_in(k)] = total.astype(jnp.bfloat16)
        row_send("r", h, t, 3, k, high, ways(h, t)[1][1])

    def row(h, t, k):
        arrived(("r", h, t, k), stage_in.at[h, t, pl.ds(0, 2), :, pl.ds(k * SLOTS * ROWS, SLOTS * ROWS)])
        cols = cols_in(k)
        total = gbuf[h, t, 0, :, cols] + received(h, t, 1, cols, both) + received(h, t, 3, cols, both)
        if t == 1:
            z_stage[h, k] = total.astype(z_stage.dtype)
            send(("zr", h, k), scatter, z_stage.at[h, k], z_in.at[h, k], over_z)
        else:
            gbuf[h, t, 0, :, cols] = total

    def zadd(h, k):
        arrived(("zr", h, k), z_in.at[h, k])
        gbuf[h, 0, 0, :, cols_in(k)] += z_in[h, k].astype(jnp.float32)

    def own_slot(h, q, rows):
        return gbuf[h, 0, 0, rows, cols_of(q)]

    def half_slot(h, q, rows):
        return (h, 0, 0, pl.ds(rows.start, WIDE // 2), pl.ds(q * ROWS, ROWS))

    def one_send(name, h, q, rows, to, value):
        stage[h, 0, 0, rows, cols_of(q)] = value.astype(jnp.bfloat16)
        where = half_slot(h, q, rows)
        send((name, h), scatter, stage.at[where], stage_in.at[where], to)

    def sum_send(h, n, to, value):
        wide[h, n] = value
        send(("sum", h), sums, wide.at[h, n], wide_in.at[h, n], to)

    def cfar(h):
        one_send("cf+", h, 2, low, ways(h, 0)[0][0], own_slot(h, 2, low))
        one_send("cf-", h, 2, high, ways(h, 0)[0][1], own_slot(h, 2, high))

    def cn1(h):
        one_send("c", h, 1, high, ways(h, 0)[0][0], own_slot(h, 1, high))

    def cn3(h):
        one_send("c", h, 3, low, ways(h, 0)[0][1], own_slot(h, 3, low))

    def cn1b(h):
        arrived(("cf+", h), stage_in.at[half_slot(h, 2, low)])
        sum_send(h, 0, ways(h, 0)[0][0], own_slot(h, 1, low) + received(h, 0, 0, cols_of(2), low))

    def cn3b(h):
        arrived(("cf-", h), stage_in.at[half_slot(h, 2, high)])
        sum_send(h, 1, ways(h, 0)[0][1], own_slot(h, 3, high) + received(h, 0, 0, cols_of(2), high))

    def finish(h):
        arrived(("c", h), stage_in.at[h, 0, 0, :, pl.ds(0, ROWS)])
        arrived(("sum", h), wide_in.at[h])
        own = own_slot(h, 0, both)
        into_low = wide_in[h, 0] + received(h, 0, 0, cols_of(3), low)
        into_high = received(h, 0, 0, cols_of(1), high) + wide_in[h, 1]
        grad_out[:, h * WIDE : h * WIDE + WIDE // 2] = (own[low] + into_low).T
        grad_out[:, h * WIDE + WIDE // 2 : (h + 1) * WIDE] = (own[high] + into_high).T

    def hids():
        @pl.loop(0, 32)
        def _(n):
            pltpu.make_async_remote_copy(
                src_ref=hidden.at[:, columns(2 * chip_of(n) + 1 - c)],
                dst_ref=hid.at[pl.ds(TOK, TOK), columns(n)],
                send_sem=hid_sem.at[1],
                recv_sem=hid_sem.at[2],
                device_id=sibling,
                device_id_type=MESH,
            ).start()

    mine, theirs = hid.at[pl.ds(0, TOK)], hid.at[pl.ds(TOK, TOK)]

    def hid_wait():
        taken(hid_sem.at[0], mine)
        taken(hid_sem.at[2], theirs)

    def chosen(n, rows):
        first = frags[n, pl.ds(2 * rows.start, rows.size, stride=2), :]
        second = frags[n, pl.ds(2 * rows.start + 1, rows.size, stride=2), :]
        return jnp.where(index[0] == 0, first, second)

    def rep():
        loads[2].wait()
        loads[3].wait()
        for n in range(4):
            rows = pl.ds(n * QUARTER, QUARTER)
            own_local = chosen(1, rows)
            local[rows, :] = own_local
            diff[rows, :] = chosen(0, rows) - own_local
        for k, to in zip((1, 2, 3), reps):
            send("rep", summed, diff.at[pl.ds(((r + k) % 4) * QUARTER, QUARTER)], rep_in.at[k - 1], to)

    def rep2():
        arrived("rep", rep_in)
        own_rows = pl.ds(r * QUARTER, QUARTER)
        delta[own_rows, :] = (diff[own_rows, :] + rep_in[0] + rep_in[1] + rep_in[2]) * 0.25
        for k, to in zip((1, 2, 3), reps):
            send("rep out", spread, delta.at[own_rows], delta.at[own_rows], to)

    stores = [
        pltpu.make_async_copy(outer.at[n], dst, out_sem.at[n])
        for n, dst in enumerate((global_out, moment_out, mixed_out))
    ]

    def repf():
        loads[4].wait()
        arrived("rep out", rep_in)
        for n in range(4):
            rows = pl.ds(n * QUARTER, QUARTER)
            step = delta[rows, :]
            outer_moment = 0.9 * chosen(2, rows) + step
            outer_global = chosen(0, rows) - 0.7 * (0.9 * outer_moment + step)
            outer[0, rows, :] = outer_global
            outer[1, rows, :] = outer_moment
            outer[2, rows, :] = 0.5 * local[rows, :] + 0.5 * outer_global
        for store in stores:
            store.start()

    steps = dict(
        zsend=zsend, own=own, nextp=nextp, nextm=nextm, far=far, passp=passp, passm=passm, keys=keys, swap=swap,
        deltas=deltas, grad=grad, rfar=rfar, rn1=rn1, rn3=rn3, rn1b=rn1b, rn3b=rn3b, row=row, zadd=zadd, cfar=cfar,
        cn1=cn1, cn3=cn3, cn1b=cn1b, cn3b=cn3b, finish=finish, hids=hids, hid=hid_wait, kgt=kgt, rep=rep, rep2=rep2, repf=repf,
    )
    for name, *where in ORDER:
        steps[name](*where)
    assert len(arrivals) == ARRIVALS
    for group, as_large in (
        (gather, wts.at[:, pl.ds(0, 31)]),
        (scatter, wts.at[:, pl.ds(0, 30)]),
        (sums, wide_in),
        (keys_swap, acc_in),
        (delta_swap, dlt.at[:, :, pl.ds(0, TOK)]),
        (summed, rep_in),
        (spread, rep_in),
    ):
        taken(send_sem.at[group], as_large)
    taken(hid_sem.at[1], mine)
    for store in stores:
        store.wait()


def project(index, hidden, master, key_grad, glob, local, moment):
    vmem, anywhere = pl.BlockSpec(memory_space=pltpu.VMEM), pl.BlockSpec(memory_space=pl.ANY)
    f32, bf16 = jnp.float32, jnp.bfloat16
    part = (4 * QUARTER, 128)
    row = (PARTS, 2, 4, WIDE, 4 * ROWS)
    return pl.pallas_call(
        kernel,
        out_shape=(
            jax.ShapeDtypeStruct((ROWS, PARTS * WIDE), f32),
            *[jax.ShapeDtypeStruct(part, f32)] * 3,
        ),
        in_specs=[pl.BlockSpec(memory_space=pltpu.SMEM), *[anywhere] * 6],
        out_specs=(vmem, *[anywhere] * 3),
        scratch_shapes=[
            pltpu.VMEM((2 * TOK, 32 * ROWS), bf16),
            pltpu.VMEM((ROWS, PARTS * WIDE), f32),
            pltpu.VMEM((TOK, PARTS * WIDE), bf16),
            pltpu.VMEM((PARTS * WIDE, TOK), f32),
            pltpu.VMEM((PARTS, 32, WIDE, ROWS), bf16),
            pltpu.VMEM((PARTS, WIDE, 2 * TOK), f32),
            pltpu.VMEM((PARTS, WIDE, TOK), f32),
            pltpu.VMEM((PARTS, WIDE, 2 * TOK), bf16),
            pltpu.VMEM(row, f32),
            pltpu.VMEM(row, bf16),
            pltpu.VMEM(row, bf16),
            pltpu.VMEM((PARTS, 4 // SLOTS, WIDE, SLOTS * ROWS), bf16),
            pltpu.VMEM((PARTS, 4 // SLOTS, WIDE, SLOTS * ROWS), bf16),
            pltpu.VMEM((PARTS, 2, WIDE // 2, ROWS), f32),
            pltpu.VMEM((PARTS, 2, WIDE // 2, ROWS), f32),
            pltpu.VMEM((3, 8 * QUARTER, 128), f32),
            pltpu.VMEM(part, f32),
            pltpu.VMEM(part, f32),
            pltpu.VMEM((3, QUARTER, 128), f32),
            pltpu.VMEM(part, f32),
            pltpu.VMEM((3, *part), f32),
            pltpu.SemaphoreType.DMA((7,)),
            pltpu.SemaphoreType.DMA((ARRIVALS,)),
            pltpu.SemaphoreType.DMA((3,)),
            pltpu.SemaphoreType.DMA((5,)),
            pltpu.SemaphoreType.DMA((3,)),
        ],
        compiler_params=pltpu.CompilerParams(
            collective_id=0, has_side_effects=True, vmem_limit_bytes=56 * 2**20
        ),
        name="project",
    )(index, hidden, master, key_grad, glob, local, moment)


def last_kernel(*refs):
    ins, outs, states, outer, in_sem, out_sem = refs[:7], refs[7:13], *refs[13:]
    held = [states.at[n] for n in range(4)] + [outer.at[n] for n in range(3)]
    results = [states.at[n] for n in range(4, 7)] + [outer.at[n] for n in range(3)]
    loads = [pltpu.make_async_copy(src, dst, in_sem.at[n]) for n, (src, dst) in enumerate(zip(ins, held))]
    stores = [pltpu.make_async_copy(src, dst, out_sem.at[n]) for n, (src, dst) in enumerate(zip(results, outs))]
    for load in loads:
        load.start()
    for load in loads[:4]:
        load.wait()
    gradient, weights = states[0], states[1]
    first_new = 0.9 * states[2] + 0.1 * gradient
    second_new = 0.95 * states[3] + 0.05 * gradient * gradient
    first_hat = first_new / (1.0 - 0.9**10)
    second_hat = second_new / (1.0 - 0.95**10)
    states[4] = weights - 0.01 * (first_hat / (jnp.sqrt(second_hat) + 1e-08) + 0.1 * weights)
    states[5] = first_new
    states[6] = second_new
    for store in stores[:3]:
        store.start()
    for load, store in zip(loads[4:], stores[3:]):
        load.wait()
        store.start()
    for store in stores:
        store.wait()


def last(grad, master, first, second, *outer):
    anywhere = pl.BlockSpec(memory_space=pl.ANY)
    return pl.pallas_call(
        last_kernel,
        out_shape=tuple(jax.ShapeDtypeStruct(v.shape, jnp.float32) for v in (master, first, second, *outer)),
        in_specs=[anywhere] * 7,
        out_specs=(anywhere,) * 6,
        scratch_shapes=[
            pltpu.VMEM((7, *master.shape), jnp.float32),
            pltpu.VMEM((3, *outer[0].shape), jnp.float32),
            pltpu.SemaphoreType.DMA((7,)),
            pltpu.SemaphoreType.DMA((6,)),
        ],
        compiler_params=pltpu.CompilerParams(vmem_limit_bytes=56 * 2**20),
        name="last",
    )(grad, master, first, second, *outer)


def rows_of(fragments):
    return fragments.reshape(2, -1, 128).transpose(1, 0, 2).reshape(-1, 128)


def shards(
    hidden,
    master,
    moment_first,
    moment_second,
    key_grad,
    frag_global,
    frag_local,
    frag_moment,
    frag_index,
):
    grad, *outer = project(
        frag_index,
        hidden[0],
        master[0],
        key_grad[0],
        rows_of(frag_global),
        rows_of(frag_local[0]),
        rows_of(frag_moment),
    )
    weights_new, first_new, second_new, *outer = last(grad, master[0], moment_first[0], moment_second[0], *outer)
    outer_global, outer_moment, mixed_local = (part.reshape(-1) for part in outer)
    return (
        weights_new[None],
        first_new[None],
        second_new[None],
        outer_global,
        outer_moment,
        mixed_local[None],
    )


def solution(mesh):
    placed = (
        P("replica", "fsdp", None),
        P("replica", "fsdp", None),
        P("replica", "fsdp", None),
        P("replica", "fsdp", None),
        P("replica", "fsdp", None),
        P(None, "fsdp"),
        P("replica", None, "fsdp"),
        P(None, "fsdp"),
        P(),
    )
    return jax.shard_map(
        shards,
        mesh=mesh,
        in_specs=placed,
        out_specs=(
            P("replica", "fsdp", None),
            P("replica", "fsdp", None),
            P("replica", "fsdp", None),
            P("fsdp"),
            P("fsdp"),
            P("replica", "fsdp"),
        ),
        check_vma=False,
    )
```

time: 78.3 us -> 66.6 us (0.85)
  Pallas kernels: 76.9 us -> 65 us
    pallas_call x1, Pallas kernels: 74 us -> 62.1 us  [project(): pl.pallas_call(kernel, out_shape=(jax.ShapeDtypeStruct((ROWS, PARTS * WID...]
where the time goes in v3:
time: 66.6 us; the launch traced here: 66.3 us
  Pallas kernels  65 us (98%)
  between operations  1.29 us (2%)
    pallas_call x1, Pallas kernels, project(): pl.pallas_call(kernel, out_shape=(jax.ShapeDtypeStruct((ROWS, PARTS * WID...  62.1 us
    pallas_call x1, Pallas kernels, last(): pl.pallas_call(last_kernel, out_shape=tuple((jax.ShapeDtypeStruct(v.shape...  2.91 us

profile of v3, /device:TPU:32, one launch (start us, length us, event | category | flops | bytes accessed | tf_op | source)
XLA Modules:
  0.0 66.3 jit_solution(4442795724372816161)
XLA Ops:
  1.3 62.1 %project.1 = (f32[128,512]{1,0:T(8,128)}, f32[1024,128]{1,0:T(8,128)}, f32[1024,128]{1,0:T(8,128)}, f32[1024,128]{1,0:T(8,128)}) custom-call(s32[1]{0:T(128)S(6)} %copy.18.index, bf16[384,8192]{1,0:T(8,128)(2,1)} %bitcast.26, f32[128,512]{1,0:T(8,128)} %bitcast.30, bf16[384,512]{1,0:T(8,128)(2,1)} %bitcast.32, f32[2048,128]{1,0:T(8,128)} %bitcast.27, ...), custom_call_target="tpu_custom_call" | custom-call | tf_op jit(solution)/shard_map/project/pallas_call | solution.py:618
  63.3 2.9 %last.1 = (f32[128,512]{1,0:T(8,128)}, f32[128,512]{1,0:T(8,128)}, f32[128,512]{1,0:T(8,128)}, f32[1024,128]{1,0:T(8,128)}, f32[1024,128]{1,0:T(8,128)}, /*index=5*/f32[1024,128]{1,0:T(8,128)}) custom-call(f32[128,512]{1,0:T(8,128)} %get-tuple-element.16.refs_0_, f32[128,512]{1,0:T(8,128)} %bitcast.31, f32[128,512]{1,0:T(8,128)} %bitcast.33, ...), custom_call_target="tpu_custom_call" | custom-call | tf_op jit(solution)/shard_map/last/pallas_call | solution.py:690

commit v4 on v3

--- a/solution.py
+++ b/solution.py
@@ -281,9 +281,9 @@
             (
                 (master_hbm, master),
                 (key_grad_hbm, key_grad),
-                (glob_hbm, frags.at[0]),
-                (local_hbm, frags.at[1]),
-                (moment_hbm, frags.at[2]),
+                (glob_hbm, frags.at[0, pl.ds(0, 8 * QUARTER)]),
+                (local_hbm, frags.at[1, pl.ds(0, 8 * QUARTER)]),
+                (moment_hbm, frags.at[2, pl.ds(0, 8 * QUARTER)]),
             )
         )
     ]
@@ -639,7 +639,7 @@
             pltpu.VMEM((PARTS, 4 // SLOTS, WIDE, SLOTS * ROWS), bf16),
             pltpu.VMEM((PARTS, 2, WIDE // 2, ROWS), f32),
             pltpu.VMEM((PARTS, 2, WIDE // 2, ROWS), f32),
-            pltpu.VMEM((3, 8 * QUARTER, 128), f32),
+            pltpu.VMEM((3, 8 * QUARTER + 8, 128), f32),
             pltpu.VMEM(part, f32),
             pltpu.VMEM(part, f32),
             pltpu.VMEM((3, QUARTER, 128), f32),

time: 66.6 us -> 66.6 us (level)
  no operation moved by 1% of the time
where the time goes in v4:
time: 66.6 us; the launch traced here: 66.3 us
  Pallas kernels  65 us (98%)
  between operations  1.29 us (2%)
    pallas_call x1, Pallas kernels, project(): pl.pallas_call(kernel, out_shape=(jax.ShapeDtypeStruct((ROWS, PARTS * WID...  62.1 us
    pallas_call x1, Pallas kernels, last(): pl.pallas_call(last_kernel, out_shape=tuple((jax.ShapeDtypeStruct(v.shape...  2.91 us

profile of v4, /device:TPU:32, one launch (start us, length us, event | category | flops | bytes accessed | tf_op | source)
XLA Modules:
  0.0 66.3 jit_solution(18427611576097234019)
XLA Ops:
  1.3 62.1 %project.1 = (f32[128,512]{1,0:T(8,128)}, f32[1024,128]{1,0:T(8,128)}, f32[1024,128]{1,0:T(8,128)}, f32[1024,128]{1,0:T(8,128)}) custom-call(s32[1]{0:T(128)S(6)} %copy.18.index, bf16[384,8192]{1,0:T(8,128)(2,1)} %bitcast.26, f32[128,512]{1,0:T(8,128)} %bitcast.30, bf16[384,512]{1,0:T(8,128)(2,1)} %bitcast.32, f32[2048,128]{1,0:T(8,128)} %bitcast.27, ...), custom_call_target="tpu_custom_call" | custom-call | tf_op jit(solution)/shard_map/project/pallas_call | solution.py:618
  63.4 2.9 %last.1 = (f32[128,512]{1,0:T(8,128)}, f32[128,512]{1,0:T(8,128)}, f32[128,512]{1,0:T(8,128)}, f32[1024,128]{1,0:T(8,128)}, f32[1024,128]{1,0:T(8,128)}, /*index=5*/f32[1024,128]{1,0:T(8,128)}) custom-call(f32[128,512]{1,0:T(8,128)} %get-tuple-element.16.refs_0_, f32[128,512]{1,0:T(8,128)} %bitcast.31, f32[128,512]{1,0:T(8,128)} %bitcast.33, ...), custom_call_target="tpu_custom_call" | custom-call | tf_op jit(solution)/shard_map/last/pallas_call | solution.py:690
